TPU v7x, 32 devices: a whole 2x2x4 slice. The times are simulated.
32 devices in a mesh: row: 8 (over z, x), feat: 4 (over y, core).
Axes of the slice: x: 2, y: 2, z: 4, core: 2. Of those that a mesh axis runs over, the one named last changes fastest.
Arguments:
- predictor: float32 [16384], P(('row', 'feat')), may hold values from -3 to 3
- events: int32 [16384], P(('row', 'feat')), may hold values 0 or 1
- tie_groups: int32 [16384], P(('row', 'feat')), may hold values from 7 to 16383, as said below
- node_ids: int32 [16384], P('row'), may hold values from 0 to 7
- bin_index: int32 [512, 16384], P('feat', 'row'), may hold values from 0 to 255
Outputs:
- gradient: float32 [16384], P(('row', 'feat'))
- hessian: float32 [16384], P(('row', 'feat'))
- split_gain: float32 [8, 512, 256], P(None, 'feat', 'row')
Inputs may be any that keep to these rules, and one draw needn't show every extreme that they name: tie_groups never falls along the rows; each value names a run of 1 to 8 consecutive rows, some run has exactly 8, and a new run begins at every multiple of 8 rows.
All inputs are finite; a program needn't handle non-finite values. No bound on the sum of `events` on one device may be relied on, other than what follows from the above.
Results may differ from a plain program's by a relative error of at most 0.0003.
The roundings to bfloat16 on the way count: a program that leaves them out, or rounds other values in their place, can miss the bound.
Values may be sent and summed in bfloat16 or wider, within the bound.
A program may use at most 64 MiB of HBM per device.

v0:
```python
import math

import jax
import jax.numpy as jnp
from jax import lax
from jax.sharding import PartitionSpec as P

BINS = 256
NODES = 8


def carried_in(part, axis, combine, identity, reverse):
    count = lax.axis_size(axis)
    place = lax.axis_index(axis)
    ahead = count - 1 - place if reverse else place
    gathered = jax.tree.map(lambda a: lax.all_gather(a, axis), part)
    state = jax.tree.map(lambda a, e: jnp.zeros_like(a) + jnp.asarray(e, a.dtype), part, identity)

    def one(hop, state):
        source = count - 1 - hop if reverse else hop
        return combine(
            state, jax.tree.map(lambda a: lax.dynamic_index_in_dim(a, source, 0, False), gathered)
        )

    return lax.fori_loop(0, ahead, one, state)


def group_bounds(tie_groups):
    length = tie_groups.shape[0]
    row_index = jnp.arange(length, dtype=jnp.int32)
    change = tie_groups[1:] != tie_groups[:-1]
    begins = jnp.concatenate([jnp.ones((1,), jnp.bool_), change])
    finish = jnp.concatenate([change, jnp.ones((1,), jnp.bool_)])
    first_row = lax.cummax(jnp.where(begins, row_index, 0), axis=0)
    last_row = lax.cummin(jnp.where(finish, row_index, length - 1), axis=0, reverse=True)
    return (first_row, last_row)


def add_values(earlier, later_value):
    return jax.tree.map(jnp.add, earlier, later_value)


def shards(predictor, events, tie_groups, node_ids, bin_index):
    hazard_exp = jnp.exp(predictor)
    suffix = jnp.cumsum(hazard_exp[::-1])[::-1]
    later_sum = carried_in(suffix[0], ("row", "feat"), add_values, jnp.zeros((), jnp.float32), True)
    first_row, last_row = group_bounds(tie_groups)
    risk_sum = (suffix + later_sum)[first_row]
    failed = events.astype(jnp.float32)
    weight_one = failed / risk_sum
    weight_two = failed / (risk_sum * risk_sum)
    cum_one = jnp.cumsum(weight_one)
    cum_two = jnp.cumsum(weight_two)
    before_one, before_two = carried_in(
        (cum_one[-1], cum_two[-1]),
        ("row", "feat"),
        add_values,
        (jnp.zeros((), jnp.float32), jnp.zeros((), jnp.float32)),
        False,
    )
    hazard_one = (cum_one + before_one)[last_row]
    hazard_two = (cum_two + before_two)[last_row]
    gradient = hazard_exp * hazard_one - failed
    hessian = hazard_exp * hazard_one - hazard_exp * hazard_exp * hazard_two
    stats = jnp.stack([gradient, hessian]).astype(jnp.bfloat16)
    levels = jnp.arange(NODES, dtype=jnp.int32)
    bin_levels = jnp.arange(BINS, dtype=jnp.int32)
    feat_count = bin_index.shape[0]
    feat_block = math.gcd(feat_count, 8)
    portion = lax.all_gather(stats, "feat", axis=1, tiled=True)
    row_count = portion.shape[1]
    node_mask = (node_ids[None, :] == levels[:, None]).astype(jnp.bfloat16)
    weighted = (node_mask[:, None, :] * portion[None, :, :]).reshape(NODES * 2, row_count)
    grouped = bin_index.reshape(feat_count // feat_block, feat_block, row_count)

    def one_block(columns):
        onehot = (columns[:, :, None] == bin_levels).astype(jnp.bfloat16)
        return jnp.einsum("cl,flb->cfb", weighted, onehot, preferred_element_type=jnp.float32)

    blocks = lax.map(one_block, grouped)
    hist = blocks.transpose(1, 0, 2, 3).reshape(NODES * 2, feat_count, BINS)
    summed = lax.psum(jnp.sum(hist, axis=2), "row")
    totals = summed.reshape(NODES, 2, feat_count, 1)
    left_flat = lax.psum_scatter(jnp.cumsum(hist, axis=2), "row", scatter_dimension=2, tiled=True)
    left_sums = left_flat.reshape(NODES, 2, feat_count, left_flat.shape[2])
    grad_left = left_sums[:, 0]
    hess_left = left_sums[:, 1]
    grad_all = totals[:, 0]
    hess_all = totals[:, 1]
    split_gain = (
        grad_left * grad_left / (hess_left + 1.0)
        + (grad_all - grad_left) ** 2 / (hess_all - hess_left + 1.0)
        - grad_all * grad_all / (hess_all + 1.0)
    )
    return (gradient, hessian, split_gain)


def solution(mesh):
    return jax.shard_map(
        shards,
        mesh=mesh,
        in_specs=(
            P(("row", "feat")),
            P(("row", "feat")),
            P(("row", "feat")),
            P("row"),
            P("feat", "row"),
        ),
        out_specs=(P(("row", "feat")), P(("row", "feat")), P(None, "feat", "row")),
        check_vma=False,
    )
```

profile of v0, /device:TPU:0, one launch (start us, length us, event | category | flops | bytes accessed | tf_op | source)
XLA Modules:
  0.0 389.0 jit_solution(3176436987066565841)
XLA Ops:
  9.7 42.0 %all-reduce = f32[32]{0:T(128)S(1)} all-reduce(f32[32]{0:T(128)S(1)} %slice_dynamic-update-slice_fusion.2), channel_id=1, replica_groups=mesh['row'=8,'feat'=4] {'row','feat'}, use_global_device_ids=true, to_apply=%add | all-reduce | flops 32 | bytes 256
  51.7 38.4 %while.35 = (s32[]{:T(128)}, f32[]{:T(128)}, s32[]{:T(128)}, f32[32]{0:T(128)S(1)}, s32[]{:T(128)}, /*index=5*/s32[]{:T(128)}, s32[]{:T(128)}, s32[]{:T(128)}) while((s32[]{:T(128)}, f32[]{:T(128)}, s32[]{:T(128)}, f32[32]{0:T(128)S(1)}, s32[]{:T(128)}, /*index=5*/s32[]{:T(128)}, s32[]{:T(128)}, s32[]{:T(128)}) %tuple.67), condition=%wide.region_3.4_spmd, body=%wide.region_2.3_spmd.sunk | while | flops 7 | bytes 163 | solution.py:25
  90.8 3.5 gather_fusion
  95.9 36.8 %all-reduce.3 = (f32[32]{0:T(128)S(1)}, f32[32]{0:T(128)S(1)}) all-reduce(f32[32]{0:T(128)S(1)} %slice_dynamic-update-slice_fusion.1, f32[32]{0:T(128)S(1)} %slice_dynamic-update-slice_fusion), channel_id=1, replica_groups=mesh['row'=8,'feat'=4] {'row','feat'}, use_global_device_ids=true, to_apply=%add.1 | all-reduce | flops 64 | bytes 512
  143.0 10.5 %all_gather.15 = bf16[2,2048]{1,0:T(2,128)(2,1)S(1)} all-gather(bf16[2,512]{1,0:T(2,128)(2,1)S(1)} %pad_maximum_fusion), channel_id=1, replica_groups=mesh['row'=8,'feat'=4] {'feat'}, dimensions={1}, use_global_device_ids=true | all-gather | bytes 10240 | tf_op jit(solution)/shard_map/all_gather | solution.py:70
  153.5 79.7 %while.37 = (s32[]{:T(128)}, f32[16,16,8,256]{3,1,2,0:T(8,128)S(1)}, s32[16,8,2048]{2,1,0:T(8,128)}, bf16[2,2048]{1,0:T(2,128)(2,1)S(1)}, bf16[8,2048]{1,0:T(8,128)(2,1)S(1)}, /*index=5*/s32[]{:T(128)}) while((s32[]{:T(128)}, f32[16,16,8,256]{3,1,2,0:T(8,128)S(1)}, s32[16,8,2048]{2,1,0:T(8,128)}, ...), condition=%wide.region_15.16_spmd.clone, body=%wide.region_14.15_spmd.clone.sunk | while | flops 138444800 | bytes 630869 | solution.py:80
  154.5 4.0 %fusion.23 = f32[16,16,8,256]{3,1,2,0:T(8,128)S(1)} fusion(f32[16,16,8,256]{3,1,2,0:T(8,128)S(1)} %get-tuple-element.338, s32[]{:T(128)S(6)} %copy.41, bf16[16,2048,1]{1,0,2:T(8,128)(2,1)S(1)} %reshape.248, s32[8,2048]{1,0:T(8,128)S(1)} %dynamic-slice_bitcast_fusion.2), kind=kOutput, calls=%fused_computation.9.clone.1 | convolution fusion | flops 138412032 | bytes 262148 | tf_op jit(solution)/shard_map/while/body/eval_jaxpr/cl,flb->cfb/dot_general | solution.py:78
  159.4 4.0 %fusion.23 = f32[16,16,8,256]{3,1,2,0:T(8,128)S(1)} fusion(f32[16,16,8,256]{3,1,2,0:T(8,128)S(1)} %get-tuple-element.338, s32[]{:T(128)S(6)} %copy.41, bf16[16,2048,1]{1,0,2:T(8,128)(2,1)S(1)} %reshape.248, s32[8,2048]{1,0:T(8,128)S(1)} %dynamic-slice_bitcast_fusion.2), kind=kOutput, calls=%fused_computation.9.clone.1 | convolution fusion | flops 138412032 | bytes 262148 | tf_op jit(solution)/shard_map/while/body/eval_jaxpr/cl,flb->cfb/dot_general | solution.py:78
  164.4 4.0 %fusion.23 = f32[16,16,8,256]{3,1,2,0:T(8,128)S(1)} fusion(f32[16,16,8,256]{3,1,2,0:T(8,128)S(1)} %get-tuple-element.338, s32[]{:T(128)S(6)} %copy.41, bf16[16,2048,1]{1,0,2:T(8,128)(2,1)S(1)} %reshape.248, s32[8,2048]{1,0:T(8,128)S(1)} %dynamic-slice_bitcast_fusion.2), kind=kOutput, calls=%fused_computation.9.clone.1 | convolution fusion | flops 138412032 | bytes 262148 | tf_op jit(solution)/shard_map/while/body/eval_jaxpr/cl,flb->cfb/dot_general | solution.py:78
  169.4 4.0 %fusion.23 = f32[16,16,8,256]{3,1,2,0:T(8,128)S(1)} fusion(f32[16,16,8,256]{3,1,2,0:T(8,128)S(1)} %get-tuple-element.338, s32[]{:T(128)S(6)} %copy.41, bf16[16,2048,1]{1,0,2:T(8,128)(2,1)S(1)} %reshape.248, s32[8,2048]{1,0:T(8,128)S(1)} %dynamic-slice_bitcast_fusion.2), kind=kOutput, calls=%fused_computation.9.clone.1 | convolution fusion | flops 138412032 | bytes 262148 | tf_op jit(solution)/shard_map/while/body/eval_jaxpr/cl,flb->cfb/dot_general | solution.py:78
  174.4 4.0 %fusion.23 = f32[16,16,8,256]{3,1,2,0:T(8,128)S(1)} fusion(f32[16,16,8,256]{3,1,2,0:T(8,128)S(1)} %get-tuple-element.338, s32[]{:T(128)S(6)} %copy.41, bf16[16,2048,1]{1,0,2:T(8,128)(2,1)S(1)} %reshape.248, s32[8,2048]{1,0:T(8,128)S(1)} %dynamic-slice_bitcast_fusion.2), kind=kOutput, calls=%fused_computation.9.clone.1 | convolution fusion | flops 138412032 | bytes 262148 | tf_op jit(solution)/shard_map/while/body/eval_jaxpr/cl,flb->cfb/dot_general | solution.py:78
  179.4 4.0 %fusion.23 = f32[16,16,8,256]{3,1,2,0:T(8,128)S(1)} fusion(f32[16,16,8,256]{3,1,2,0:T(8,128)S(1)} %get-tuple-element.338, s32[]{:T(128)S(6)} %copy.41, bf16[16,2048,1]{1,0,2:T(8,128)(2,1)S(1)} %reshape.248, s32[8,2048]{1,0:T(8,128)S(1)} %dynamic-slice_bitcast_fusion.2), kind=kOutput, calls=%fused_computation.9.clone.1 | convolution fusion | flops 138412032 | bytes 262148 | tf_op jit(solution)/shard_map/while/body/eval_jaxpr/cl,flb->cfb/dot_general | solution.py:78
  184.3 4.0 %fusion.23 = f32[16,16,8,256]{3,1,2,0:T(8,128)S(1)} fusion(f32[16,16,8,256]{3,1,2,0:T(8,128)S(1)} %get-tuple-element.338, s32[]{:T(128)S(6)} %copy.41, bf16[16,2048,1]{1,0,2:T(8,128)(2,1)S(1)} %reshape.248, s32[8,2048]{1,0:T(8,128)S(1)} %dynamic-slice_bitcast_fusion.2), kind=kOutput, calls=%fused_computation.9.clone.1 | convolution fusion | flops 138412032 | bytes 262148 | tf_op jit(solution)/shard_map/while/body/eval_jaxpr/cl,flb->cfb/dot_general | solution.py:78
  189.3 4.0 %fusion.23 = f32[16,16,8,256]{3,1,2,0:T(8,128)S(1)} fusion(f32[16,16,8,256]{3,1,2,0:T(8,128)S(1)} %get-tuple-element.338, s32[]{:T(128)S(6)} %copy.41, bf16[16,2048,1]{1,0,2:T(8,128)(2,1)S(1)} %reshape.248, s32[8,2048]{1,0:T(8,128)S(1)} %dynamic-slice_bitcast_fusion.2), kind=kOutput, calls=%fused_computation.9.clone.1 | convolution fusion | flops 138412032 | bytes 262148 | tf_op jit(solution)/shard_map/while/body/eval_jaxpr/cl,flb->cfb/dot_general | solution.py:78
  194.3 4.0 %fusion.23 = f32[16,16,8,256]{3,1,2,0:T(8,128)S(1)} fusion(f32[16,16,8,256]{3,1,2,0:T(8,128)S(1)} %get-tuple-element.338, s32[]{:T(128)S(6)} %copy.41, bf16[16,2048,1]{1,0,2:T(8,128)(2,1)S(1)} %reshape.248, s32[8,2048]{1,0:T(8,128)S(1)} %dynamic-slice_bitcast_fusion.2), kind=kOutput, calls=%fused_computation.9.clone.1 | convolution fusion | flops 138412032 | bytes 262148 | tf_op jit(solution)/shard_map/while/body/eval_jaxpr/cl,flb->cfb/dot_general | solution.py:78
  199.3 4.0 %fusion.23 = f32[16,16,8,256]{3,1,2,0:T(8,128)S(1)} fusion(f32[16,16,8,256]{3,1,2,0:T(8,128)S(1)} %get-tuple-element.338, s32[]{:T(128)S(6)} %copy.41, bf16[16,2048,1]{1,0,2:T(8,128)(2,1)S(1)} %reshape.248, s32[8,2048]{1,0:T(8,128)S(1)} %dynamic-slice_bitcast_fusion.2), kind=kOutput, calls=%fused_computation.9.clone.1 | convolution fusion | flops 138412032 | bytes 262148 | tf_op jit(solution)/shard_map/while/body/eval_jaxpr/cl,flb->cfb/dot_general | solution.py:78
  204.3 4.0 %fusion.23 = f32[16,16,8,256]{3,1,2,0:T(8,128)S(1)} fusion(f32[16,16,8,256]{3,1,2,0:T(8,128)S(1)} %get-tuple-element.338, s32[]{:T(128)S(6)} %copy.41, bf16[16,2048,1]{1,0,2:T(8,128)(2,1)S(1)} %reshape.248, s32[8,2048]{1,0:T(8,128)S(1)} %dynamic-slice_bitcast_fusion.2), kind=kOutput, calls=%fused_computation.9.clone.1 | convolution fusion | flops 138412032 | bytes 262148 | tf_op jit(solution)/shard_map/while/body/eval_jaxpr/cl,flb->cfb/dot_general | solution.py:78
  209.2 4.0 %fusion.23 = f32[16,16,8,256]{3,1,2,0:T(8,128)S(1)} fusion(f32[16,16,8,256]{3,1,2,0:T(8,128)S(1)} %get-tuple-element.338, s32[]{:T(128)S(6)} %copy.41, bf16[16,2048,1]{1,0,2:T(8,128)(2,1)S(1)} %reshape.248, s32[8,2048]{1,0:T(8,128)S(1)} %dynamic-slice_bitcast_fusion.2), kind=kOutput, calls=%fused_computation.9.clone.1 | convolution fusion | flops 138412032 | bytes 262148 | tf_op jit(solution)/shard_map/while/body/eval_jaxpr/cl,flb->cfb/dot_general | solution.py:78
  214.2 4.0 %fusion.23 = f32[16,16,8,256]{3,1,2,0:T(8,128)S(1)} fusion(f32[16,16,8,256]{3,1,2,0:T(8,128)S(1)} %get-tuple-element.338, s32[]{:T(128)S(6)} %copy.41, bf16[16,2048,1]{1,0,2:T(8,128)(2,1)S(1)} %reshape.248, s32[8,2048]{1,0:T(8,128)S(1)} %dynamic-slice_bitcast_fusion.2), kind=kOutput, calls=%fused_computation.9.clone.1 | convolution fusion | flops 138412032 | bytes 262148 | tf_op jit(solution)/shard_map/while/body/eval_jaxpr/cl,flb->cfb/dot_general | solution.py:78
  219.2 4.0 %fusion.23 = f32[16,16,8,256]{3,1,2,0:T(8,128)S(1)} fusion(f32[16,16,8,256]{3,1,2,0:T(8,128)S(1)} %get-tuple-element.338, s32[]{:T(128)S(6)} %copy.41, bf16[16,2048,1]{1,0,2:T(8,128)(2,1)S(1)} %reshape.248, s32[8,2048]{1,0:T(8,128)S(1)} %dynamic-slice_bitcast_fusion.2), kind=kOutput, calls=%fused_computation.9.clone.1 | convolution fusion | flops 138412032 | bytes 262148 | tf_op jit(solution)/shard_map/while/body/eval_jaxpr/cl,flb->cfb/dot_general | solution.py:78
  224.2 4.0 %fusion.23 = f32[16,16,8,256]{3,1,2,0:T(8,128)S(1)} fusion(f32[16,16,8,256]{3,1,2,0:T(8,128)S(1)} %get-tuple-element.338, s32[]{:T(128)S(6)} %copy.41, bf16[16,2048,1]{1,0,2:T(8,128)(2,1)S(1)} %reshape.248, s32[8,2048]{1,0:T(8,128)S(1)} %dynamic-slice_bitcast_fusion.2), kind=kOutput, calls=%fused_computation.9.clone.1 | convolution fusion | flops 138412032 | bytes 262148 | tf_op jit(solution)/shard_map/while/body/eval_jaxpr/cl,flb->cfb/dot_general | solution.py:78
  229.2 4.0 %fusion.23 = f32[16,16,8,256]{3,1,2,0:T(8,128)S(1)} fusion(f32[16,16,8,256]{3,1,2,0:T(8,128)S(1)} %get-tuple-element.338, s32[]{:T(128)S(6)} %copy.41, bf16[16,2048,1]{1,0,2:T(8,128)(2,1)S(1)} %reshape.248, s32[8,2048]{1,0:T(8,128)S(1)} %dynamic-slice_bitcast_fusion.2), kind=kOutput, calls=%fused_computation.9.clone.1 | convolution fusion | flops 138412032 | bytes 262148 | tf_op jit(solution)/shard_map/while/body/eval_jaxpr/cl,flb->cfb/dot_general | solution.py:78
  243.0 91.5 %psum.7 = f32[8,2,128,1]{2,1,0,3:T(2,128)S(1)} all-reduce(f32[8,2,128,1]{2,1,0,3:T(2,128)S(1)} %reshape.208), channel_id=1, replica_groups=mesh['row'=8,'feat'=4] {'row'}, use_global_device_ids=true, to_apply=%region_20.21 | all-reduce | flops 2048 | bytes 16384 | tf_op jit(solution)/shard_map/psum | solution.py:82
  334.5 45.9 %reduce-scatter.2.cloned.1.call-done = f32[16,128,32]{1,2,0:T(8,128)} async-done(((f32[16,128,256]{1,2,0:T(8,128)}), f32[16,128,32]{1,2,0:T(8,128)}) %reduce-scatter.2.cloned.1.call-update) | async-done | bytes 262160 | tf_op jit(solution)/shard_map/reduce_scatter | solution.py:84
  (151 shorter events, 60.4 us)
Async XLA Ops:
  7.2 87.2 %copy-start.2 = (s32[512]{0:T(512)S(1)}, s32[512]{0:T(512)}, u32[]{:S(2)}) copy-start(s32[512]{0:T(512)} %param.12) | copy-start | bytes 6148
  7.2 373.3 %reduce-scatter.2.cloned.1.call-start = ((), (), s32[]{:S(2)}) async-start(), calls=%async_computation.1 | async-start | bytes 2359296 | tf_op jit(solution)/shard_map/reduce_scatter | solution.py:84
  135.3 7.0 %copy-start.1 = (f32[512]{0:T(512)S(1)}, f32[512]{0:T(512)}, u32[]{:S(2)}) copy-start(f32[512]{0:T(512)} %param.11) | copy-start | bytes 6148
  135.3 18.1 %copy-start = (s32[2048]{0:T(1024)S(1)}, s32[2048]{0:T(1024)}, u32[]{:S(2)}) copy-start(s32[2048]{0:T(1024)} %param.14) | copy-start | bytes 24580
Sparse Core Ops, SparseCore 0:
  242.5 137.8 reduce-scatter.1
where the time goes:
time: 392 us; the launch traced here: 389 us
  blocking collectives  181 us (46%)
  matrix products  64 us (16%)
  local copies, waits for them, and re-layouts  52.8 us (13%)
  waiting for transfers between devices  46 us (12%)
  loops' own time  20.2 us (5%)
  between operations  14.2 us (4%)
  other arithmetic  11 us (3%)
    psum x1, blocking collectives, shards(): summed = lax.psum(jnp.sum(hist, axis=2), 'row')  91.5 us
    unnamed x2, blocking collectives  78.8 us
    dot_general x16, matrix products, one_block(): jnp.einsum('cl,flb->cfb', weighted, onehot, preferred_element_type=jnp.fl...  64 us
    reduce_scatter x1, waiting for transfers between devices, shards(): lax.psum_scatter(jnp.cumsum(hist, axis=2), 'row', scatter_dimension=2, ti...  45.9 us
    another operation x2, loops' own time, carried_in(): return lax.fori_loop(0, ahead, one, state)  20 us
    dynamic_slice x31, local copies, waits for them, and re-layouts, one(): lax.dynamic_index_in_dim(a, source, 0, False)  18.5 us
    eq x16, local copies, waits for them, and re-layouts, one_block(): onehot = (columns[:, :, None] == bin_levels).astype(jnp.bfloat16)  13.6 us
    all_gather x1, blocking collectives, shards(): portion = lax.all_gather(stats, 'feat', axis=1, tiled=True)  10.5 us
  transfers between devices with their start and end apart: 1, of which 1 were waited for; matrix products, arithmetic and copies ran while one was open for 0% of the time, Pallas kernels for 0%

commit v1 on v0

v1 whole, which is shorter than its diff:
```python
import functools

import jax
import jax.numpy as jnp
from jax import lax
from jax.experimental import pallas as pl
from jax.experimental.pallas import tpu as pltpu
from jax.sharding import PartitionSpec as P

BINS = 256
NODES = 8
LANES = 128
HIGH = 4
LOW = BINS // HIGH
CHANNELS = 2 * NODES
GROUP = 4
BLOCKS = 4
MESH = pl.DeviceIdType.MESH
EXACT = lax.Precision.HIGHEST


def partner(me, step, count):
    other = me
    bit = 1
    while bit < count:
        other = other + ((step // bit) % 2) * bit * (1 - 2 * ((me // bit) % 2))
        bit *= 2
    return other


def triangle(rows, columns, keep):
    a = lax.broadcasted_iota(jnp.int32, (rows, columns), 0)
    b = lax.broadcasted_iota(jnp.int32, (rows, columns), 1)
    return keep(a, b).astype(jnp.float32)


def exact_dot(a, b):
    return jnp.dot(a, b, precision=EXACT, preferred_element_type=jnp.float32)


def fill(value, known, step):
    for distance in (1, 2, 4):
        shift = distance if step > 0 else LANES - distance
        value = jnp.where(known > 0, value, pltpu.roll(value, shift, 1))
        known = jnp.maximum(known, pltpu.roll(known, shift, 1))
    return value


def cox(score, code):
    rows = score.shape[0]
    hazard_exp = jnp.exp(score)
    tie = code // 2
    failed = (code - 2 * tie).astype(jnp.float32)
    lane = lax.broadcasted_iota(jnp.int32, (rows, LANES), 1)
    begins = ((lane % 8 == 0) | (tie != pltpu.roll(tie, 1, 1))).astype(jnp.float32)
    finish = pltpu.roll(begins, LANES - 1, 1)
    lane_suffix = exact_dot(hazard_exp, triangle(LANES, LANES, lambda a, b: a >= b))
    whole = jnp.broadcast_to(lane_suffix[:, :1], (rows, LANES))
    suffix = lane_suffix + exact_dot(triangle(rows, rows, lambda a, b: b > a), whole)
    risk_sum = fill(suffix, begins, 1)
    weight_one = failed / risk_sum
    weight_two = failed / (risk_sum * risk_sum)
    upper = triangle(LANES, LANES, lambda a, b: a <= b)
    earlier = triangle(rows, rows, lambda a, b: b < a)

    def running(weight):
        within = exact_dot(weight, upper)
        whole = jnp.broadcast_to(within[:, LANES - 1 :], (rows, LANES))
        return fill(within + exact_dot(earlier, whole), finish, -1)

    hazard_one = running(weight_one)
    hazard_two = running(weight_two)
    gradient = hazard_exp * hazard_one - failed
    hessian = hazard_exp * hazard_one - hazard_exp * hazard_exp * hazard_two
    return gradient, hessian


def kernel(
    nr, nf, pred_ref, event_ref, tie_ref, node_ref, bin_ref, grad_ref, hess_ref, gain_ref,
    pay, nodes, bin_send, bin_recv, gain_send, gain_recv, acc, turned, score, code, grads, hesss,
    levelled, pay_send_sem, pay_sem, node_send_sem, node_sem, bin_send_sem, bin_sem, gain_send_sem, gain_sem,
):
    my_row = lax.axis_index("row")
    my_feat = lax.axis_index("feat")
    me = my_row * nf + my_feat
    count = nr * nf
    quarter = pred_ref.shape[0]
    blocks = bin_ref.shape[1] // LANES
    own = bin_ref.shape[0] // nr
    tile = bin_send.shape[2]
    slice_bins = BINS // nr

    def coords(device):
        return (device // nf, device % nf)

    barrier = pltpu.get_barrier_semaphore()

    def greet(step, carry):
        other = (me + step) % count
        pl.semaphore_signal(barrier, inc=1, device_id=coords(other), device_id_type=MESH)
        return carry

    lax.fori_loop(1, count, greet, 0)

    pay[me, 0:quarter, :] = pred_ref[...]
    pay[me, quarter : 2 * quarter, :] = (tie_ref[...] * 2 + event_ref[...]).astype(jnp.float32)
    nodes[my_row] = node_ref[...].astype(jnp.float32).astype(jnp.bfloat16)

    def pack(block, carry):
        lanes = pl.ds(pl.multiple_of(block * LANES, LANES), LANES)
        for target in range(nr):
            part = bin_ref[target * own : (target + 1) * own, lanes].astype(jnp.float32)
            if own < tile:
                part = jnp.concatenate([part, jnp.zeros((tile - own, LANES), jnp.float32)], axis=0)
            bin_send[target, block] = part.astype(jnp.bfloat16)
        return carry

    lax.fori_loop(0, blocks, pack, 0)
    pl.semaphore_wait(barrier, count - 1)

    def pay_copy(other):
        return pltpu.make_async_remote_copy(
            src_ref=pay.at[me], dst_ref=pay.at[me], send_sem=pay_send_sem, recv_sem=pay_sem,
            device_id=coords(other), device_id_type=MESH,
        )

    def node_copy(step):
        other = partner(my_row, step, nr)
        return pltpu.make_async_remote_copy(
            src_ref=nodes.at[my_row], dst_ref=nodes.at[my_row],
            send_sem=node_send_sem, recv_sem=node_sem,
            device_id=(other, my_feat), device_id_type=MESH,
        )

    def bin_copy(step):
        other = partner(my_row, step, nr)
        return pltpu.make_async_remote_copy(
            src_ref=bin_send.at[other], dst_ref=bin_recv.at[my_row],
            send_sem=bin_send_sem.at[step], recv_sem=bin_sem.at[step],
            device_id=(other, my_feat), device_id_type=MESH,
        )

    def gain_copy(step):
        other = partner(my_row, step, nr)
        return pltpu.make_async_remote_copy(
            src_ref=gain_send.at[other], dst_ref=gain_recv.at[my_row],
            send_sem=gain_send_sem.at[step], recv_sem=gain_sem.at[step],
            device_id=(other, my_feat), device_id_type=MESH,
        )

    def send_pay(step, carry):
        pay_copy((me + step) % count).start()
        return carry

    lax.fori_loop(1, count, send_pay, 0)

    def send_nodes(step, carry):
        node_copy(step).start()
        return carry

    lax.fori_loop(1, nr, send_nodes, 0)

    def send_bins(step, carry):
        bin_copy(nr - step).start()
        return carry

    lax.fori_loop(1, nr, send_bins, 0)

    bin_recv[my_row] = bin_send[my_row]
    acc[...] = jnp.zeros_like(acc)

    others = pl.ds(0, count - 1)
    pltpu.make_async_copy(pay.at[others], pay.at[others], pay_sem).wait()

    def spread(device, carry):
        rows = pl.ds(device * quarter, quarter)
        score[rows, :] = pay[device, 0:quarter, :]
        code[rows, :] = pay[device, quarter : 2 * quarter, :].astype(jnp.int32)
        return carry

    lax.fori_loop(0, count, spread, 0)
    gradient, hessian = cox(score[...], code[...])
    grads[...] = gradient
    hesss[...] = hessian
    mine = pl.ds(me * quarter, quarter)
    grad_ref[...] = grads[mine, :]
    hess_ref[...] = hesss[mine, :]

    row_others = pl.ds(0, nr - 1)
    pltpu.make_async_copy(nodes.at[row_others], nodes.at[row_others], node_sem).wait()
    for source in range(nr):
        levelled[source * blocks : (source + 1) * blocks, :] = nodes[source].astype(jnp.float32)

    levels = lax.broadcasted_iota(jnp.int32, (NODES, LANES), 0).astype(jnp.float32)
    low_levels = [
        (lax.broadcasted_iota(jnp.int32, (16, LANES), 0) + 16 * part).astype(jnp.float32).astype(jnp.bfloat16)
        for part in range(LOW // 16)
    ]
    one = jnp.ones((16, LANES), jnp.bfloat16)
    zero = jnp.zeros((16, LANES), jnp.bfloat16)
    groups = -(-own // GROUP)

    def one_source(step, carry):
        source = partner(my_row, step, nr)

        @pl.when(step > 0)
        def _():
            bin_copy(step).wait_recv()

        def one_chunk(chunk, carry):
            weights, highs, lows = [], [], []
            for inner in range(BLOCKS):
                block = chunk * BLOCKS + inner
                row = pl.ds(source * blocks + block, 1)
                is_node = jnp.broadcast_to(levelled[row, :], (NODES, LANES)) == levels
                weight = jnp.concatenate(
                    [
                        jnp.where(is_node, jnp.broadcast_to(grads[row, :], (NODES, LANES)), 0.0),
                        jnp.where(is_node, jnp.broadcast_to(hesss[row, :], (NODES, LANES)), 0.0),
                    ],
                    axis=0,
                )
                weights.append(weight.astype(jnp.bfloat16))
                bins = bin_recv[source, block].astype(jnp.float32)
                high = jnp.floor(bins * (1.0 / LOW))
                highs.append(high)
                lows.append(bins - high * LOW)
            for group in range(groups):
                left, right = [], []
                for inner in range(GROUP):
                    feature = group * GROUP + inner
                    high = [jnp.broadcast_to(h[feature : feature + 1], (16, LANES)).astype(jnp.bfloat16) for h in highs]
                    low = [jnp.broadcast_to(l[feature : feature + 1], (16, LANES)).astype(jnp.bfloat16) for l in lows]
                    for level in range(HIGH):
                        left.append(
                            jnp.concatenate(
                                [jnp.where(h == level, w, zero) for h, w in zip(high, weights)], axis=1
                            )
                        )
                    for level in low_levels:
                        right.append(
                            jnp.concatenate([jnp.where(l <= level, one, zero) for l in low], axis=1)
                        )
                acc[group] += lax.dot_general(
                    jnp.concatenate(left, axis=0),
                    jnp.concatenate(right, axis=0),
                    (((1,), (1,)), ((), ())),
                    preferred_element_type=jnp.float32,
                )
            return carry

        lax.fori_loop(0, blocks // BLOCKS, one_chunk, 0)
        return carry

    lax.fori_loop(0, nr, one_source, 0)

    for feature in range(own):
        group, inner = divmod(feature, GROUP)
        columns = slice(inner * LOW, (inner + 1) * LOW)
        lefts, running = [], [None, None]
        for level in range(HIGH):
            for stat in range(2):
                top = ((inner * HIGH + level) * 2 + stat) * NODES
                part = acc[group, top : top + NODES, columns]
                if level:
                    part = part + running[stat]
                running[stat] = jnp.broadcast_to(part[:, LOW - 1 :], (NODES, LOW))
                lefts.append(part)
        grad_all, hess_all = running
        base = grad_all * grad_all / (hess_all + 1.0)
        for level in range(HIGH):
            grad_left, hess_left = lefts[2 * level], lefts[2 * level + 1]
            rest = grad_all - grad_left
            gain = (
                grad_left * grad_left / (hess_left + 1.0)
                + rest * rest / (hess_all - hess_left + 1.0)
                - base
            )
            turned[level, pl.ds(feature, NODES, stride=own), 0:LOW] = gain

    for level in range(HIGH):
        flipped = jnp.transpose(turned[level])
        for part in range(LOW // slice_bins):
            gain_send[level * (LOW // slice_bins) + part] = flipped[part * slice_bins : (part + 1) * slice_bins]

    def send_gain(step, carry):
        gain_copy(nr - step).start()
        return carry

    lax.fori_loop(1, nr, send_gain, 0)
    gain_recv[my_row] = gain_send[my_row]

    def take_gain(step, carry):
        gain_copy(step).wait_recv()
        return carry

    lax.fori_loop(1, nr, take_gain, 0)
    for source in range(nr):
        for node in range(NODES):
            gain_ref[node, :, source * own : (source + 1) * own] = gain_recv[source, :, node * own : (node + 1) * own]

    def settle(step, carry):
        bin_copy(step).wait_send()
        gain_copy(step).wait_send()
        return carry

    lax.fori_loop(1, nr, settle, 0)
    pltpu.make_async_copy(pay.at[others], pay.at[others], pay_send_sem).wait()
    pltpu.make_async_copy(nodes.at[row_others], nodes.at[row_others], node_send_sem).wait()


def shards(nr, nf, predictor, events, tie_groups, node_ids, bin_index):
    length = predictor.shape[0]
    quarter = length // LANES
    rows = node_ids.shape[0]
    features = bin_index.shape[0]
    own = features // nr
    blocks = rows // LANES
    tile = -(-own // 16) * 16
    groups = -(-own // GROUP)
    all_rows = nr * blocks
    slice_bins = BINS // nr
    vmem = pl.BlockSpec(memory_space=pltpu.VMEM)
    f32, bf16 = jnp.float32, jnp.bfloat16
    gradient, hessian, gain = pl.pallas_call(
        functools.partial(kernel, nr, nf),
        out_shape=(
            jax.ShapeDtypeStruct((quarter, LANES), f32),
            jax.ShapeDtypeStruct((quarter, LANES), f32),
            jax.ShapeDtypeStruct((NODES, slice_bins, features), f32),
        ),
        in_specs=[vmem] * 5,
        out_specs=(vmem,) * 3,
        scratch_shapes=[
            pltpu.VMEM((nr * nf, 2 * quarter, LANES), f32),
            pltpu.VMEM((nr, blocks, LANES), bf16),
            pltpu.VMEM((nr, blocks, tile, LANES), bf16),
            pltpu.VMEM((nr, blocks, tile, LANES), bf16),
            pltpu.VMEM((nr, slice_bins, LANES), f32),
            pltpu.VMEM((nr, slice_bins, LANES), f32),
            pltpu.VMEM((groups, GROUP * HIGH * CHANNELS, GROUP * LOW), f32),
            pltpu.VMEM((HIGH, LANES, LANES), f32),
            pltpu.VMEM((all_rows, LANES), f32),
            pltpu.VMEM((all_rows, LANES), jnp.int32),
            pltpu.VMEM((all_rows, LANES), f32),
            pltpu.VMEM((all_rows, LANES), f32),
            pltpu.VMEM((all_rows, LANES), f32),
            pltpu.SemaphoreType.DMA,
            pltpu.SemaphoreType.DMA,
            pltpu.SemaphoreType.DMA,
            pltpu.SemaphoreType.DMA,
            pltpu.SemaphoreType.DMA((nr,)),
            pltpu.SemaphoreType.DMA((nr,)),
            pltpu.SemaphoreType.DMA((nr,)),
            pltpu.SemaphoreType.DMA((nr,)),
        ],
        compiler_params=pltpu.CompilerParams(
            collective_id=0, has_side_effects=True, vmem_limit_bytes=48 * 1024 * 1024
        ),
    )(
        predictor.reshape(quarter, LANES),
        events.reshape(quarter, LANES),
        tie_groups.reshape(quarter, LANES),
        node_ids.reshape(blocks, LANES),
        bin_index,
    )
    return gradient.reshape(length), hessian.reshape(length), gain.transpose(0, 2, 1)


def solution(mesh):
    return jax.shard_map(
        functools.partial(shards, mesh.shape["row"], mesh.shape["feat"]),
        mesh=mesh,
        in_specs=(
            P(("row", "feat")),
            P(("row", "feat")),
            P(("row", "feat")),
            P("row"),
            P("feat", "row"),
        ),
        out_specs=(P(("row", "feat")), P(("row", "feat")), P(None, "feat", "row")),
        check_vma=False,
    )
```

time: 392 us -> 46.1 us (0.12)
  blocking collectives: 181 us -> 0 us
  matrix products: 64 us -> 0 us
  local copies, waits for them, and re-layouts: 52.8 us -> 4.42 us
  waiting for transfers between devices: 46 us -> 0 us
  Pallas kernels: 0 us -> 40.8 us
  loops' own time: 20.2 us -> 0 us
  between operations: 14.2 us -> 0.67 us
  other arithmetic: 11 us -> 0 us
    psum x1 -> x0, blocking collectives: 91.5 us -> none  [shards(): summed = lax.psum(jnp.sum(hist, axis=2), 'row')]
    unnamed x2 -> x0, blocking collectives: 78.8 us -> none
    dot_general x16 -> x0, matrix products: 64 us -> none  [one_block(): jnp.einsum('cl,flb->cfb', weighted, onehot, preferred_element_type=jnp.fl...]
    reduce_scatter x1 -> x0, waiting for transfers between devices: 45.9 us -> none  [shards(): lax.psum_scatter(jnp.cumsum(hist, axis=2), 'row', scatter_dimension=2, ti...]
    pallas_call x0 -> x1, Pallas kernels: none -> 40.8 us  [shards(): pl.pallas_call(functools.partial(kernel, nr, nf), out_shape=(jax.ShapeDty...]
    another operation x3 -> x0, loops' own time: 20.2 us -> none  [the longest x2 20 us: carried_in(): return lax.fori_loop(0, ahead, one, state)]
    dynamic_slice x31 -> x0, local copies, waits for them, and re-layouts: 18.5 us -> none  [one(): lax.dynamic_index_in_dim(a, source, 0, False)]
    eq x16 -> x0, local copies, waits for them, and re-layouts: 13.6 us -> none  [one_block(): onehot = (columns[:, :, None] == bin_levels).astype(jnp.bfloat16)]
  transfers between devices with their start and end apart: 1 -> 0, of which waited for: 1 -> 0; matrix products, arithmetic and copies ran while one was open for 0% -> 0% of each run, Pallas kernels for 0% -> 0%
where the time goes in v1:
time: 46.1 us; the launch traced here: 45.9 us
  Pallas kernels  40.8 us (89%)
  local copies, waits for them, and re-layouts  4.42 us (10%)
  between operations  0.67 us (1%)
    pallas_call x1, Pallas kernels, shards(): pl.pallas_call(functools.partial(kernel, nr, nf), out_shape=(jax.ShapeDty...  40.8 us
    unnamed x13, local copies, waits for them, and re-layouts  4.42 us

profile of v1, /device:TPU:0, one launch (start us, length us, event | category | flops | bytes accessed | tf_op | source)
XLA Modules:
  0.0 45.9 jit_solution(10281929663042486778)
XLA Ops:
  0.6 0.0 copy-start.4
  0.6 0.0 copy-start.3
  0.7 0.0 copy-start.2
  0.7 0.7 %copy-done.4 = s32[512]{0:T(512)S(1)} copy-done((s32[512]{0:T(512)S(1)}, s32[512]{0:T(512)}, u32[]{:S(2)}) %copy-start.4) | copy-done | bytes 2072
  1.3 0.0 copy-done.3
  1.3 0.0 copy-done.2
  1.3 0.0 copy-start
  1.3 1.2 %copy-done = s32[128,2048]{1,0:T(8,128)S(1)} copy-done((s32[128,2048]{1,0:T(8,128)S(1)}, s32[128,2048]{1,0:T(8,128)}, u32[]{:S(2)}) %copy-start) | copy-done | bytes 1048600
  2.6 0.0 copy-start.1
  2.6 0.7 %copy-done.1 = s32[2048]{0:T(1024)S(1)} copy-done((s32[2048]{0:T(1024)S(1)}, s32[2048]{0:T(1024)}, u32[]{:S(2)}) %copy-start.1) | copy-done | bytes 8216
  3.3 40.8 %shard_map.76 = (f32[4,128]{1,0:T(4,128)S(1)}, f32[4,128]{1,0:T(4,128)S(1)}, f32[8,32,128]{2,1,0:T(8,128)S(1)}) custom-call(f32[4,128]{1,0:T(4,128)S(1)} %bitcast.9, s32[4,128]{1,0:T(4,128)S(1)} %bitcast.10, s32[4,128]{1,0:T(4,128)S(1)} %bitcast.11, s32[16,128]{1,0:T(8,128)S(1)} %bitcast.8, s32[128,2048]{1,0:T(8,128)S(1)} %copy-done), custom_call_target="tpu_custom_call" | custom-call | tf_op jit(solution)/shard_map/pallas_call | solution.py:325
  44.1 0.6 %copy.11 = f32[512]{0:T(512)} copy(f32[512]{0:T(512)S(1)} %bitcast.13) | data formatting | bytes 4096
  44.6 0.6 %copy.12 = f32[512]{0:T(512)} copy(f32[512]{0:T(512)S(1)} %bitcast.12) | data formatting | bytes 4096
  45.2 0.7 %copy.13 = f32[8,128,32]{1,2,0:T(8,128)} copy(f32[8,128,32]{1,2,0:T(8,128)S(1)} %bitcast.7) | data formatting | bytes 262144
Async XLA Ops:
  0.6 0.7 %copy-start.4 = (s32[512]{0:T(512)S(1)}, s32[512]{0:T(512)}, u32[]{:S(2)}) copy-start(s32[512]{0:T(512)} %param.7) | copy-start | bytes 6148
  0.6 0.7 %copy-start.3 = (s32[512]{0:T(512)S(1)}, s32[512]{0:T(512)}, u32[]{:S(2)}) copy-start(s32[512]{0:T(512)} %param.6) | copy-start | bytes 6148
  0.7 0.7 %copy-start.2 = (f32[512]{0:T(512)S(1)}, f32[512]{0:T(512)}, u32[]{:S(2)}) copy-start(f32[512]{0:T(512)} %param.5) | copy-start | bytes 6148
  1.3 1.2 %copy-start = (s32[128,2048]{1,0:T(8,128)S(1)}, s32[128,2048]{1,0:T(8,128)}, u32[]{:S(2)}) copy-start(s32[128,2048]{1,0:T(8,128)} %bin_ref.1) | copy-start | bytes 3145732
  2.6 0.7 %copy-start.1 = (s32[2048]{0:T(1024)S(1)}, s32[2048]{0:T(1024)}, u32[]{:S(2)}) copy-start(s32[2048]{0:T(1024)} %param.8) | copy-start | bytes 24580

commit v2 on v1

--- a/solution.py
+++ b/solution.py
@@ -13,7 +13,7 @@
 HIGH = 4
 LOW = BINS // HIGH
 CHANNELS = 2 * NODES
-GROUP = 4
+GROUP = 2
 BLOCKS = 4
 MESH = pl.DeviceIdType.MESH
 EXACT = lax.Precision.HIGHEST
@@ -76,9 +76,10 @@
 
 
 def kernel(
-    nr, nf, pred_ref, event_ref, tie_ref, node_ref, bin_ref, grad_ref, hess_ref, gain_ref,
+    nr, nf, pred_hbm, event_hbm, tie_hbm, node_hbm, bin_hbm, grad_ref, hess_ref, gain_ref,
+    pred_ref, event_ref, tie_ref, node_ref, bin_ref, highs, lows, weights,
     pay, nodes, bin_send, bin_recv, gain_send, gain_recv, acc, turned, score, code, grads, hesss,
-    levelled, pay_send_sem, pay_sem, node_send_sem, node_sem, bin_send_sem, bin_sem, gain_send_sem, gain_sem,
+    levelled, in_sem, pay_send_sem, pay_sem, node_send_sem, node_sem, bin_send_sem, bin_sem, gain_send_sem, gain_sem,
 ):
     my_row = lax.axis_index("row")
     my_feat = lax.axis_index("feat")
@@ -93,6 +94,14 @@
     def coords(device):
         return (device // nf, device % nf)
 
+    reads = [
+        pltpu.make_async_copy(source, target, in_sem.at[place])
+        for place, (source, target) in enumerate(
+            [(pred_hbm, pred_ref), (event_hbm, event_ref), (tie_hbm, tie_ref), (node_hbm, node_ref), (bin_hbm, bin_ref)]
+        )
+    ]
+    for read in reads:
+        read.start()
     barrier = pltpu.get_barrier_semaphore()
 
     def greet(step, carry):
@@ -102,9 +111,13 @@
 
     lax.fori_loop(1, count, greet, 0)
 
+    for read in reads[:4]:
+        read.wait()
     pay[me, 0:quarter, :] = pred_ref[...]
     pay[me, quarter : 2 * quarter, :] = (tie_ref[...] * 2 + event_ref[...]).astype(jnp.float32)
     nodes[my_row] = node_ref[...].astype(jnp.float32).astype(jnp.bfloat16)
+
+    reads[4].wait()
 
     def pack(block, carry):
         lanes = pl.ds(pl.multiple_of(block * LANES, LANES), LANES)
@@ -207,34 +220,40 @@
         def _():
             bin_copy(step).wait_recv()
 
+        for block in range(blocks):
+            row = pl.ds(source * blocks + block, 1)
+            is_node = jnp.broadcast_to(levelled[row, :], (NODES, LANES)) == levels
+            weight = jnp.concatenate(
+                [
+                    jnp.where(is_node, jnp.broadcast_to(grads[row, :], (NODES, LANES)), 0.0),
+                    jnp.where(is_node, jnp.broadcast_to(hesss[row, :], (NODES, LANES)), 0.0),
+                ],
+                axis=0,
+            )
+            weights[block] = weight.astype(jnp.bfloat16)
+            bins = bin_recv[source, block].astype(jnp.float32)
+            high = jnp.floor(bins * (1.0 / LOW))
+            highs[block] = high
+            lows[block] = bins - high * LOW
+
         def one_chunk(chunk, carry):
-            weights, highs, lows = [], [], []
-            for inner in range(BLOCKS):
-                block = chunk * BLOCKS + inner
-                row = pl.ds(source * blocks + block, 1)
-                is_node = jnp.broadcast_to(levelled[row, :], (NODES, LANES)) == levels
-                weight = jnp.concatenate(
-                    [
-                        jnp.where(is_node, jnp.broadcast_to(grads[row, :], (NODES, LANES)), 0.0),
-                        jnp.where(is_node, jnp.broadcast_to(hesss[row, :], (NODES, LANES)), 0.0),
-                    ],
-                    axis=0,
-                )
-                weights.append(weight.astype(jnp.bfloat16))
-                bins = bin_recv[source, block].astype(jnp.float32)
-                high = jnp.floor(bins * (1.0 / LOW))
-                highs.append(high)
-                lows.append(bins - high * LOW)
+            here = [chunk * BLOCKS + inner for inner in range(BLOCKS)]
+            weight = [weights[block] for block in here]
+
+            def row_of(ref, block, feature):
+                row = ref[block, feature : feature + 1, :]
+                return jnp.broadcast_to(row, (16, LANES)).astype(jnp.bfloat16)
+
             for group in range(groups):
                 left, right = [], []
                 for inner in range(GROUP):
                     feature = group * GROUP + inner
-                    high = [jnp.broadcast_to(h[feature : feature + 1], (16, LANES)).astype(jnp.bfloat16) for h in highs]
-                    low = [jnp.broadcast_to(l[feature : feature + 1], (16, LANES)).astype(jnp.bfloat16) for l in lows]
+                    high = [row_of(highs, block, feature) for block in here]
+                    low = [row_of(lows, block, feature) for block in here]
                     for level in range(HIGH):
                         left.append(
                             jnp.concatenate(
-                                [jnp.where(h == level, w, zero) for h, w in zip(high, weights)], axis=1
+                                [jnp.where(h == level, w, zero) for h, w in zip(high, weight)], axis=1
                             )
                         )
                     for level in low_levels:
@@ -329,9 +348,17 @@
             jax.ShapeDtypeStruct((quarter, LANES), f32),
             jax.ShapeDtypeStruct((NODES, slice_bins, features), f32),
         ),
-        in_specs=[vmem] * 5,
+        in_specs=[pl.BlockSpec(memory_space=pltpu.HBM)] * 5,
         out_specs=(vmem,) * 3,
         scratch_shapes=[
+            pltpu.VMEM((quarter, LANES), f32),
+            pltpu.VMEM((quarter, LANES), jnp.int32),
+            pltpu.VMEM((quarter, LANES), jnp.int32),
+            pltpu.VMEM((blocks, LANES), jnp.int32),
+            pltpu.VMEM((features, rows), jnp.int32),
+            pltpu.VMEM((blocks, tile, LANES), f32),
+            pltpu.VMEM((blocks, tile, LANES), f32),
+            pltpu.VMEM((blocks, CHANNELS, LANES), bf16),
             pltpu.VMEM((nr * nf, 2 * quarter, LANES), f32),
             pltpu.VMEM((nr, blocks, LANES), bf16),
             pltpu.VMEM((nr, blocks, tile, LANES), bf16),
@@ -345,6 +372,7 @@
             pltpu.VMEM((all_rows, LANES), f32),
             pltpu.VMEM((all_rows, LANES), f32),
             pltpu.VMEM((all_rows, LANES), f32),
+            pltpu.SemaphoreType.DMA((5,)),
             pltpu.SemaphoreType.DMA,
             pltpu.SemaphoreType.DMA,
             pltpu.SemaphoreType.DMA,
@@ -355,7 +383,7 @@
             pltpu.SemaphoreType.DMA((nr,)),
         ],
         compiler_params=pltpu.CompilerParams(
-            collective_id=0, has_side_effects=True, vmem_limit_bytes=48 * 1024 * 1024
+            collective_id=0, has_side_effects=True, vmem_limit_bytes=63 * 1024 * 1024
         ),
     )(
         predictor.reshape(quarter, LANES),

time: 46.1 us -> 45.3 us (0.983)
  local copies, waits for them, and re-layouts: 4.42 us -> 3.47 us
    unnamed x13 -> x7, local copies, waits for them, and re-layouts: 4.42 us -> 3.47 us
where the time goes in v2:
time: 45.3 us; the launch traced here: 45.1 us
  Pallas kernels  41 us (91%)
  local copies, waits for them, and re-layouts  3.47 us (8%)
  between operations  0.65 us (1%)
    pallas_call x1, Pallas kernels, shards(): pl.pallas_call(functools.partial(kernel, nr, nf), out_shape=(jax.ShapeDty...  41 us
    unnamed x7, local copies, waits for them, and re-layouts  3.47 us

profile of v2, /device:TPU:0, one launch (start us, length us, event | category | flops | bytes accessed | tf_op | source)
XLA Modules:
  0.0 45.1 jit_solution(16986851419321887383)
XLA Ops:
  0.6 41.0 %shard_map.76 = (f32[4,128]{1,0:T(4,128)}, f32[4,128]{1,0:T(4,128)}, f32[8,32,128]{2,1,0:T(8,128)}) custom-call(f32[4,128]{1,0:T(4,128)} %bitcast.9, s32[4,128]{1,0:T(4,128)} %bitcast.10, s32[4,128]{1,0:T(4,128)} %bitcast.11, s32[16,128]{1,0:T(8,128)} %bitcast.8, s32[128,2048]{1,0:T(8,128)} %bin_hbm.1), custom_call_target="tpu_custom_call" | custom-call | tf_op jit(solution)/shard_map/pallas_call | solution.py:344
  41.6 0.0 copy-start.1
  41.6 0.7 %copy-done.1 = f32[4,128]{1,0:T(4,128)S(1)} copy-done((f32[4,128]{1,0:T(4,128)S(1)}, f32[4,128]{1,0:T(4,128)}, u32[]{:S(2)}) %copy-start.1) | copy-done | bytes 2072
  42.3 0.0 copy-start
  42.3 0.6 %copy.11 = f32[512]{0:T(512)} copy(f32[512]{0:T(512)S(1)} %bitcast.13) | data formatting | bytes 4096
  42.9 0.1 copy-done
  43.0 0.6 %copy.12 = f32[512]{0:T(512)} copy(f32[512]{0:T(512)S(1)} %bitcast.12) | data formatting | bytes 4096
  43.6 1.6 %copy.13 = f32[8,128,32]{1,2,0:T(8,128)} copy(f32[8,128,32]{1,2,0:T(8,128)} %bitcast.7) | data formatting | bytes 262144
Async XLA Ops:
  41.6 0.7 %copy-start.1 = (f32[4,128]{1,0:T(4,128)S(1)}, f32[4,128]{1,0:T(4,128)}, u32[]{:S(2)}) copy-start(f32[4,128]{1,0:T(4,128)} %get-tuple-element.6) | copy-start | bytes 6148
  42.3 0.7 %copy-start = (f32[4,128]{1,0:T(4,128)S(1)}, f32[4,128]{1,0:T(4,128)}, u32[]{:S(2)}) copy-start(f32[4,128]{1,0:T(4,128)} %get-tuple-element.7) | copy-start | bytes 6148

commit v3 on v2

--- a/solution.py
+++ b/solution.py
@@ -26,6 +26,15 @@
         other = other + ((step // bit) % 2) * bit * (1 - 2 * ((me // bit) % 2))
         bit *= 2
     return other
+
+
+def step_of(place, count):
+    half = count // 2
+    odd = place % 2
+    last = place // (count - 1)
+    later = (place + count - 1) // count
+    by_turns = odd * ((place + 1) // 2) + (1 - odd) * later * (half + place // 2 - 1)
+    return (1 - last) * by_turns + last * (count - 1)
 
 
 def triangle(rows, columns, keep):
@@ -78,21 +87,17 @@
 def kernel(
     nr, nf, pred_hbm, event_hbm, tie_hbm, node_hbm, bin_hbm, grad_ref, hess_ref, gain_ref,
     pred_ref, event_ref, tie_ref, node_ref, bin_ref, highs, lows, weights,
-    pay, nodes, bin_send, bin_recv, gain_send, gain_recv, acc, turned, score, code, grads, hesss,
-    levelled, in_sem, pay_send_sem, pay_sem, node_send_sem, node_sem, bin_send_sem, bin_sem, gain_send_sem, gain_sem,
+    pay, bin_send, bin_recv, gain_send, gain_recv, acc, turned, score, code, grads, hesss,
+    levelled, in_sem, row_send_sem, row_sem, feat_send_sem, feat_sem, bin_send_sem, bin_sem, gain_send_sem, gain_sem,
 ):
     my_row = lax.axis_index("row")
     my_feat = lax.axis_index("feat")
     me = my_row * nf + my_feat
-    count = nr * nf
     quarter = pred_ref.shape[0]
     blocks = bin_ref.shape[1] // LANES
     own = bin_ref.shape[0] // nr
     tile = bin_send.shape[2]
     slice_bins = BINS // nr
-
-    def coords(device):
-        return (device // nf, device % nf)
 
     reads = [
         pltpu.make_async_copy(source, target, in_sem.at[place])
@@ -104,19 +109,25 @@
         read.start()
     barrier = pltpu.get_barrier_semaphore()
 
-    def greet(step, carry):
-        other = (me + step) % count
-        pl.semaphore_signal(barrier, inc=1, device_id=coords(other), device_id_type=MESH)
-        return carry
-
-    lax.fori_loop(1, count, greet, 0)
+    def greet_row(step, carry):
+        other = (my_row + step) % nr
+        pl.semaphore_signal(barrier, inc=1, device_id=(other, my_feat), device_id_type=MESH)
+        return carry
+
+    def greet_feat(step, carry):
+        other = (my_feat + step) % nf
+        pl.semaphore_signal(barrier, inc=1, device_id=(my_row, other), device_id_type=MESH)
+        return carry
+
+    lax.fori_loop(1, nr, greet_row, 0)
+    lax.fori_loop(1, nf, greet_feat, 0)
 
     for read in reads[:4]:
         read.wait()
-    pay[me, 0:quarter, :] = pred_ref[...]
-    pay[me, quarter : 2 * quarter, :] = (tie_ref[...] * 2 + event_ref[...]).astype(jnp.float32)
-    nodes[my_row] = node_ref[...].astype(jnp.float32).astype(jnp.bfloat16)
-
+    pay[my_feat, my_row, 0:quarter, :] = pred_ref[...]
+    pay[my_feat, my_row, quarter : 2 * quarter, :] = (tie_ref[...] * 2 + event_ref[...]).astype(jnp.float32)
+    share = node_ref[pl.ds(my_feat * quarter, quarter), :]
+    pay[my_feat, my_row, 2 * quarter : 3 * quarter, :] = share.astype(jnp.float32)
     reads[4].wait()
 
     def pack(block, carry):
@@ -129,20 +140,22 @@
         return carry
 
     lax.fori_loop(0, blocks, pack, 0)
-    pl.semaphore_wait(barrier, count - 1)
-
-    def pay_copy(other):
+    pl.semaphore_wait(barrier, nr + nf - 2)
+
+    def row_copy(step):
+        other = partner(my_row, step, nr)
+        mine = pay.at[my_feat, my_row]
         return pltpu.make_async_remote_copy(
-            src_ref=pay.at[me], dst_ref=pay.at[me], send_sem=pay_send_sem, recv_sem=pay_sem,
-            device_id=coords(other), device_id_type=MESH,
+            src_ref=mine, dst_ref=mine, send_sem=row_send_sem, recv_sem=row_sem,
+            device_id=(other, my_feat), device_id_type=MESH,
         )
 
-    def node_copy(step):
-        other = partner(my_row, step, nr)
+    def feat_copy(step):
+        other = (my_feat + step) % nf
         return pltpu.make_async_remote_copy(
-            src_ref=nodes.at[my_row], dst_ref=nodes.at[my_row],
-            send_sem=node_send_sem, recv_sem=node_sem,
-            device_id=(other, my_feat), device_id_type=MESH,
+            src_ref=pay.at[my_feat], dst_ref=pay.at[my_feat],
+            send_sem=feat_send_sem, recv_sem=feat_sem,
+            device_id=(my_row, other), device_id_type=MESH,
         )
 
     def bin_copy(step):
@@ -161,20 +174,14 @@
             device_id=(other, my_feat), device_id_type=MESH,
         )
 
-    def send_pay(step, carry):
-        pay_copy((me + step) % count).start()
-        return carry
-
-    lax.fori_loop(1, count, send_pay, 0)
-
-    def send_nodes(step, carry):
-        node_copy(step).start()
-        return carry
-
-    lax.fori_loop(1, nr, send_nodes, 0)
-
-    def send_bins(step, carry):
-        bin_copy(nr - step).start()
+    def send_row(step, carry):
+        row_copy(nr - step).start()
+        return carry
+
+    lax.fori_loop(1, nr, send_row, 0)
+
+    def send_bins(place, carry):
+        bin_copy(step_of(place, nr)).start()
         return carry
 
     lax.fori_loop(1, nr, send_bins, 0)
@@ -182,27 +189,32 @@
     bin_recv[my_row] = bin_send[my_row]
     acc[...] = jnp.zeros_like(acc)
 
-    others = pl.ds(0, count - 1)
-    pltpu.make_async_copy(pay.at[others], pay.at[others], pay_sem).wait()
-
-    def spread(device, carry):
-        rows = pl.ds(device * quarter, quarter)
-        score[rows, :] = pay[device, 0:quarter, :]
-        code[rows, :] = pay[device, quarter : 2 * quarter, :].astype(jnp.int32)
-        return carry
-
-    lax.fori_loop(0, count, spread, 0)
+    row_bytes = pay.at[0, pl.ds(0, nr - 1)]
+    feat_bytes = pay.at[pl.ds(0, nf - 1)]
+    pltpu.make_async_copy(row_bytes, row_bytes, row_sem).wait()
+
+    def send_feat(step, carry):
+        feat_copy(step).start()
+        return carry
+
+    lax.fori_loop(1, nf, send_feat, 0)
+    pltpu.make_async_copy(feat_bytes, feat_bytes, feat_sem).wait()
+
+    def spread(row, carry):
+        for feat in range(nf):
+            rows = pl.ds((row * nf + feat) * quarter, quarter)
+            score[rows, :] = pay[feat, row, 0:quarter, :]
+            code[rows, :] = pay[feat, row, quarter : 2 * quarter, :].astype(jnp.int32)
+            levelled[rows, :] = pay[feat, row, 2 * quarter : 3 * quarter, :]
+        return carry
+
+    lax.fori_loop(0, nr, spread, 0)
     gradient, hessian = cox(score[...], code[...])
     grads[...] = gradient
     hesss[...] = hessian
     mine = pl.ds(me * quarter, quarter)
     grad_ref[...] = grads[mine, :]
     hess_ref[...] = hesss[mine, :]
-
-    row_others = pl.ds(0, nr - 1)
-    pltpu.make_async_copy(nodes.at[row_others], nodes.at[row_others], node_sem).wait()
-    for source in range(nr):
-        levelled[source * blocks : (source + 1) * blocks, :] = nodes[source].astype(jnp.float32)
 
     levels = lax.broadcasted_iota(jnp.int32, (NODES, LANES), 0).astype(jnp.float32)
     low_levels = [
@@ -213,10 +225,11 @@
     zero = jnp.zeros((16, LANES), jnp.bfloat16)
     groups = -(-own // GROUP)
 
-    def one_source(step, carry):
+    def one_source(place, carry):
+        step = step_of(place, nr)
         source = partner(my_row, step, nr)
 
-        @pl.when(step > 0)
+        @pl.when(place > 0)
         def _():
             bin_copy(step).wait_recv()
 
@@ -250,12 +263,13 @@
                     feature = group * GROUP + inner
                     high = [row_of(highs, block, feature) for block in here]
                     low = [row_of(lows, block, feature) for block in here]
-                    for level in range(HIGH):
+                    for level in range(HIGH - 1):
                         left.append(
                             jnp.concatenate(
-                                [jnp.where(h == level, w, zero) for h, w in zip(high, weight)], axis=1
+                                [jnp.where(h <= level, w, zero) for h, w in zip(high, weight)], axis=1
                             )
                         )
+                    left.append(jnp.concatenate(weight, axis=1))
                     for level in low_levels:
                         right.append(
                             jnp.concatenate([jnp.where(l <= level, one, zero) for l in low], axis=1)
@@ -276,15 +290,14 @@
     for feature in range(own):
         group, inner = divmod(feature, GROUP)
         columns = slice(inner * LOW, (inner + 1) * LOW)
-        lefts, running = [], [None, None]
+        lefts, before, running = [], [None, None], [None, None]
         for level in range(HIGH):
             for stat in range(2):
                 top = ((inner * HIGH + level) * 2 + stat) * NODES
                 part = acc[group, top : top + NODES, columns]
-                if level:
-                    part = part + running[stat]
+                lefts.append(running[stat] + (part - before[stat]) if level else part)
+                before[stat] = part
                 running[stat] = jnp.broadcast_to(part[:, LOW - 1 :], (NODES, LOW))
-                lefts.append(part)
         grad_all, hess_all = running
         base = grad_all * grad_all / (hess_all + 1.0)
         for level in range(HIGH):
@@ -324,8 +337,8 @@
         return carry
 
     lax.fori_loop(1, nr, settle, 0)
-    pltpu.make_async_copy(pay.at[others], pay.at[others], pay_send_sem).wait()
-    pltpu.make_async_copy(nodes.at[row_others], nodes.at[row_others], node_send_sem).wait()
+    pltpu.make_async_copy(row_bytes, row_bytes, row_send_sem).wait()
+    pltpu.make_async_copy(feat_bytes, feat_bytes, feat_send_sem).wait()
 
 
 def shards(nr, nf, predictor, events, tie_groups, node_ids, bin_index):
@@ -359,8 +372,7 @@
             pltpu.VMEM((blocks, tile, LANES), f32),
             pltpu.VMEM((blocks, tile, LANES), f32),
             pltpu.VMEM((blocks, CHANNELS, LANES), bf16),
-            pltpu.VMEM((nr * nf, 2 * quarter, LANES), f32),
-            pltpu.VMEM((nr, blocks, LANES), bf16),
+            pltpu.VMEM((nf, nr, -(-3 * quarter // 8) * 8, LANES), f32),
             pltpu.VMEM((nr, blocks, tile, LANES), bf16),
             pltpu.VMEM((nr, blocks, tile, LANES), bf16),
             pltpu.VMEM((nr, slice_bins, LANES), f32),

time: 45.3 us -> 41.7 us (0.921)
  Pallas kernels: 41 us -> 37.4 us
    pallas_call x1, Pallas kernels: 41 us -> 37.4 us  [shards(): pl.pallas_call(functools.partial(kernel, nr, nf), out_shape=(jax.ShapeDty...]
where the time goes in v3:
time: 41.7 us; the launch traced here: 41.5 us
  Pallas kernels  37.4 us (90%)
  local copies, waits for them, and re-layouts  3.47 us (8%)
  between operations  0.65 us (2%)
    pallas_call x1, Pallas kernels, shards(): pl.pallas_call(functools.partial(kernel, nr, nf), out_shape=(jax.ShapeDty...  37.4 us
    unnamed x7, local copies, waits for them, and re-layouts  3.47 us

profile of v3, /device:TPU:0, one launch (start us, length us, event | category | flops | bytes accessed | tf_op | source)
XLA Modules:
  0.0 41.5 jit_solution(16008343414385060512)
XLA Ops:
  0.6 37.4 %shard_map.76 = (f32[4,128]{1,0:T(4,128)}, f32[4,128]{1,0:T(4,128)}, f32[8,32,128]{2,1,0:T(8,128)}) custom-call(f32[4,128]{1,0:T(4,128)} %bitcast.9, s32[4,128]{1,0:T(4,128)} %bitcast.10, s32[4,128]{1,0:T(4,128)} %bitcast.11, s32[16,128]{1,0:T(8,128)} %bitcast.8, s32[128,2048]{1,0:T(8,128)} %bin_hbm.1), custom_call_target="tpu_custom_call" | custom-call | tf_op jit(solution)/shard_map/pallas_call | solution.py:357
  38.0 0.0 copy-start.1
  38.0 0.7 %copy-done.1 = f32[4,128]{1,0:T(4,128)S(1)} copy-done((f32[4,128]{1,0:T(4,128)S(1)}, f32[4,128]{1,0:T(4,128)}, u32[]{:S(2)}) %copy-start.1) | copy-done | bytes 2072
  38.7 0.0 copy-start
  38.7 0.6 %copy.11 = f32[512]{0:T(512)} copy(f32[512]{0:T(512)S(1)} %bitcast.13) | data formatting | bytes 4096
  39.3 0.1 copy-done
  39.3 0.6 %copy.12 = f32[512]{0:T(512)} copy(f32[512]{0:T(512)S(1)} %bitcast.12) | data formatting | bytes 4096
  39.9 1.6 %copy.13 = f32[8,128,32]{1,2,0:T(8,128)} copy(f32[8,128,32]{1,2,0:T(8,128)} %bitcast.7) | data formatting | bytes 262144
Async XLA Ops:
  38.0 0.7 %copy-start.1 = (f32[4,128]{1,0:T(4,128)S(1)}, f32[4,128]{1,0:T(4,128)}, u32[]{:S(2)}) copy-start(f32[4,128]{1,0:T(4,128)} %get-tuple-element.6) | copy-start | bytes 6148
  38.7 0.7 %copy-start = (f32[4,128]{1,0:T(4,128)S(1)}, f32[4,128]{1,0:T(4,128)}, u32[]{:S(2)}) copy-start(f32[4,128]{1,0:T(4,128)} %get-tuple-element.7) | copy-start | bytes 6148

commit v4 on v3

--- a/solution.py
+++ b/solution.py
@@ -14,7 +14,7 @@
 LOW = BINS // HIGH
 CHANNELS = 2 * NODES
 GROUP = 2
-BLOCKS = 4
+BLOCKS = 8
 MESH = pl.DeviceIdType.MESH
 EXACT = lax.Precision.HIGHEST
 
@@ -128,6 +128,46 @@
     pay[my_feat, my_row, quarter : 2 * quarter, :] = (tie_ref[...] * 2 + event_ref[...]).astype(jnp.float32)
     share = node_ref[pl.ds(my_feat * quarter, quarter), :]
     pay[my_feat, my_row, 2 * quarter : 3 * quarter, :] = share.astype(jnp.float32)
+    pl.semaphore_wait(barrier, nr + nf - 2)
+
+    def row_copy(step):
+        other = partner(my_row, step, nr)
+        mine = pay.at[my_feat, my_row]
+        return pltpu.make_async_remote_copy(
+            src_ref=mine, dst_ref=mine, send_sem=row_send_sem, recv_sem=row_sem,
+            device_id=(other, my_feat), device_id_type=MESH,
+        )
+
+    def feat_copy(step):
+        other = (my_feat + step) % nf
+        return pltpu.make_async_remote_copy(
+            src_ref=pay.at[my_feat], dst_ref=pay.at[my_feat],
+            send_sem=feat_send_sem, recv_sem=feat_sem,
+            device_id=(my_row, other), device_id_type=MESH,
+        )
+
+    def bin_copy(step):
+        other = partner(my_row, step, nr)
+        return pltpu.make_async_remote_copy(
+            src_ref=bin_send.at[other], dst_ref=bin_recv.at[my_row],
+            send_sem=bin_send_sem.at[step], recv_sem=bin_sem.at[step],
+            device_id=(other, my_feat), device_id_type=MESH,
+        )
+
+    def gain_copy(step, half):
+        other = partner(my_row, step, nr)
+        return pltpu.make_async_remote_copy(
+            src_ref=gain_send.at[half, other], dst_ref=gain_recv.at[half, my_row],
+            send_sem=gain_send_sem.at[half, step], recv_sem=gain_sem.at[half, step],
+            device_id=(other, my_feat), device_id_type=MESH,
+        )
+
+    def send_row(step, carry):
+        row_copy(nr - step).start()
+        return carry
+
+    lax.fori_loop(1, nr, send_row, 0)
+
     reads[4].wait()
 
     def pack(block, carry):
@@ -140,45 +180,6 @@
         return carry
 
     lax.fori_loop(0, blocks, pack, 0)
-    pl.semaphore_wait(barrier, nr + nf - 2)
-
-    def row_copy(step):
-        other = partner(my_row, step, nr)
-        mine = pay.at[my_feat, my_row]
-        return pltpu.make_async_remote_copy(
-            src_ref=mine, dst_ref=mine, send_sem=row_send_sem, recv_sem=row_sem,
-            device_id=(other, my_feat), device_id_type=MESH,
-        )
-
-    def feat_copy(step):
-        other = (my_feat + step) % nf
-        return pltpu.make_async_remote_copy(
-            src_ref=pay.at[my_feat], dst_ref=pay.at[my_feat],
-            send_sem=feat_send_sem, recv_sem=feat_sem,
-            device_id=(my_row, other), device_id_type=MESH,
-        )
-
-    def bin_copy(step):
-        other = partner(my_row, step, nr)
-        return pltpu.make_async_remote_copy(
-            src_ref=bin_send.at[other], dst_ref=bin_recv.at[my_row],
-            send_sem=bin_send_sem.at[step], recv_sem=bin_sem.at[step],
-            device_id=(other, my_feat), device_id_type=MESH,
-        )
-
-    def gain_copy(step):
-        other = partner(my_row, step, nr)
-        return pltpu.make_async_remote_copy(
-            src_ref=gain_send.at[other], dst_ref=gain_recv.at[my_row],
-            send_sem=gain_send_sem.at[step], recv_sem=gain_sem.at[step],
-            device_id=(other, my_feat), device_id_type=MESH,
-        )
-
-    def send_row(step, carry):
-        row_copy(nr - step).start()
-        return carry
-
-    lax.fori_loop(1, nr, send_row, 0)
 
     def send_bins(place, carry):
         bin_copy(step_of(place, nr)).start()
@@ -223,9 +224,12 @@
     ]
     one = jnp.ones((16, LANES), jnp.bfloat16)
     zero = jnp.zeros((16, LANES), jnp.bfloat16)
-    groups = -(-own // GROUP)
-
-    def one_source(place, carry):
+    halves = gain_send.shape[0]
+    some = own // halves
+    width = NODES * some
+    short = slice_bins // halves
+
+    def prepare(place, carry):
         step = step_of(place, nr)
         source = partner(my_row, step, nr)
 
@@ -233,8 +237,9 @@
         def _():
             bin_copy(step).wait_recv()
 
-        for block in range(blocks):
-            row = pl.ds(source * blocks + block, 1)
+        for inner in range(blocks):
+            block = source * blocks + inner
+            row = pl.ds(block, 1)
             is_node = jnp.broadcast_to(levelled[row, :], (NODES, LANES)) == levels
             weight = jnp.concatenate(
                 [
@@ -244,20 +249,23 @@
                 axis=0,
             )
             weights[block] = weight.astype(jnp.bfloat16)
-            bins = bin_recv[source, block].astype(jnp.float32)
+            bins = bin_recv[source, inner].astype(jnp.float32)
             high = jnp.floor(bins * (1.0 / LOW))
             highs[block] = high
             lows[block] = bins - high * LOW
-
+        count_source(source, 0)
+        return carry
+
+    def count_source(source, half):
         def one_chunk(chunk, carry):
-            here = [chunk * BLOCKS + inner for inner in range(BLOCKS)]
+            here = [source * blocks + chunk * BLOCKS + inner for inner in range(BLOCKS)]
             weight = [weights[block] for block in here]
 
             def row_of(ref, block, feature):
                 row = ref[block, feature : feature + 1, :]
                 return jnp.broadcast_to(row, (16, LANES)).astype(jnp.bfloat16)
 
-            for group in range(groups):
+            for group in range(half * some // GROUP, (half + 1) * some // GROUP):
                 left, right = [], []
                 for inner in range(GROUP):
                     feature = group * GROUP + inner
@@ -283,62 +291,92 @@
             return carry
 
         lax.fori_loop(0, blocks // BLOCKS, one_chunk, 0)
-        return carry
-
-    lax.fori_loop(0, nr, one_source, 0)
-
-    for feature in range(own):
-        group, inner = divmod(feature, GROUP)
-        columns = slice(inner * LOW, (inner + 1) * LOW)
-        lefts, before, running = [], [None, None], [None, None]
+
+    def count_again(half, source, carry):
+        count_source(source, half)
+        return carry
+
+    def send_gain(half, step, carry):
+        gain_copy(nr - step, half).start()
+        return carry
+
+    def take_gain(half, step, carry):
+        gain_copy(step, half).wait_recv()
+        return carry
+
+    def split(half):
+        for place in range(some):
+            group, inner = divmod(half * some + place, GROUP)
+            columns = slice(inner * LOW, (inner + 1) * LOW)
+            lefts, before, running = [], [None, None], [None, None]
+            for level in range(HIGH):
+                for stat in range(2):
+                    top = ((inner * HIGH + level) * 2 + stat) * NODES
+                    part = acc[group, top : top + NODES, columns]
+                    lefts.append(running[stat] + (part - before[stat]) if level else part)
+                    before[stat] = part
+                    running[stat] = jnp.broadcast_to(part[:, LOW - 1 :], (NODES, LOW))
+            grad_all, hess_all = running
+            base = grad_all * grad_all / (hess_all + 1.0)
+            for level in range(HIGH):
+                grad_left, hess_left = lefts[2 * level], lefts[2 * level + 1]
+                rest = grad_all - grad_left
+                gain = (
+                    grad_left * grad_left / (hess_left + 1.0)
+                    + rest * rest / (hess_all - hess_left + 1.0)
+                    - base
+                )
+                turned[half, level, pl.ds(place, NODES, stride=some), 0:LOW] = gain
         for level in range(HIGH):
-            for stat in range(2):
-                top = ((inner * HIGH + level) * 2 + stat) * NODES
-                part = acc[group, top : top + NODES, columns]
-                lefts.append(running[stat] + (part - before[stat]) if level else part)
-                before[stat] = part
-                running[stat] = jnp.broadcast_to(part[:, LOW - 1 :], (NODES, LOW))
-        grad_all, hess_all = running
-        base = grad_all * grad_all / (hess_all + 1.0)
-        for level in range(HIGH):
-            grad_left, hess_left = lefts[2 * level], lefts[2 * level + 1]
-            rest = grad_all - grad_left
-            gain = (
-                grad_left * grad_left / (hess_left + 1.0)
-                + rest * rest / (hess_all - hess_left + 1.0)
-                - base
-            )
-            turned[level, pl.ds(feature, NODES, stride=own), 0:LOW] = gain
-
-    for level in range(HIGH):
-        flipped = jnp.transpose(turned[level])
-        for part in range(LOW // slice_bins):
-            gain_send[level * (LOW // slice_bins) + part] = flipped[part * slice_bins : (part + 1) * slice_bins]
-
-    def send_gain(step, carry):
-        gain_copy(nr - step).start()
-        return carry
-
-    lax.fori_loop(1, nr, send_gain, 0)
-    gain_recv[my_row] = gain_send[my_row]
-
-    def take_gain(step, carry):
-        gain_copy(step).wait_recv()
-        return carry
-
-    lax.fori_loop(1, nr, take_gain, 0)
-    for source in range(nr):
-        for node in range(NODES):
-            gain_ref[node, :, source * own : (source + 1) * own] = gain_recv[source, :, node * own : (node + 1) * own]
+            flipped = jnp.transpose(turned[half, level])
+            for part in range(LOW // slice_bins):
+                top = part * slice_bins
+                pieces = [flipped[top + sub * short : top + (sub + 1) * short, :width] for sub in range(halves)]
+                whole = jnp.concatenate(pieces, axis=1) if halves > 1 else flipped[top : top + slice_bins]
+                gain_send[half, level * (LOW // slice_bins) + part] = whole
+
+    def place_gain(half):
+        for source in range(nr):
+            for sub in range(halves):
+                for node in range(NODES):
+                    lanes = sub * width + node * some
+                    column = source * own + half * some
+                    gain_ref[node, sub * short : (sub + 1) * short, column : column + some] = gain_recv[
+                        half, source, :, lanes : lanes + some
+                    ]
+
+    for half in range(halves):
+        if half:
+            lax.fori_loop(0, nr, functools.partial(count_again, half), 0)
+        else:
+            lax.fori_loop(0, nr, prepare, 0)
+        split(half)
+        lax.fori_loop(1, nr, functools.partial(send_gain, half), 0)
+        gain_recv[half, my_row] = gain_send[half, my_row]
+    for half in range(halves):
+        lax.fori_loop(1, nr, functools.partial(take_gain, half), 0)
+        place_gain(half)
 
     def settle(step, carry):
         bin_copy(step).wait_send()
-        gain_copy(step).wait_send()
+        for half in range(halves):
+            gain_copy(step, half).wait_send()
         return carry
 
     lax.fori_loop(1, nr, settle, 0)
     pltpu.make_async_copy(row_bytes, row_bytes, row_send_sem).wait()
     pltpu.make_async_copy(feat_bytes, feat_bytes, feat_send_sem).wait()
+
+
+def hand_on(*refs):
+    count = len(refs) // 2
+    copies = [
+        pltpu.make_async_copy(refs[place], refs[count + place], refs[-1].at[place]) for place in range(count)
+    ]
+    for copy in copies:
+        copy.start()
+    for copy in copies:
+        copy.wait()
 
 
 def shards(nr, nf, predictor, events, tie_groups, node_ids, bin_index):
@@ -352,9 +390,10 @@
     groups = -(-own // GROUP)
     all_rows = nr * blocks
     slice_bins = BINS // nr
+    halves = 2 if own % (2 * GROUP) == 0 and NODES * own == LANES and slice_bins % 16 == 0 else 1
     vmem = pl.BlockSpec(memory_space=pltpu.VMEM)
     f32, bf16 = jnp.float32, jnp.bfloat16
-    gradient, hessian, gain = pl.pallas_call(
+    results = pl.pallas_call(
         functools.partial(kernel, nr, nf),
         out_shape=(
             jax.ShapeDtypeStruct((quarter, LANES), f32),
@@ -369,16 +408,16 @@
             pltpu.VMEM((quarter, LANES), jnp.int32),
             pltpu.VMEM((blocks, LANES), jnp.int32),
             pltpu.VMEM((features, rows), jnp.int32),
-            pltpu.VMEM((blocks, tile, LANES), f32),
-            pltpu.VMEM((blocks, tile, LANES), f32),
-            pltpu.VMEM((blocks, CHANNELS, LANES), bf16),
+            pltpu.VMEM((all_rows, tile, LANES), f32),
+            pltpu.VMEM((all_rows, tile, LANES), f32),
+            pltpu.VMEM((all_rows, CHANNELS, LANES), bf16),
             pltpu.VMEM((nf, nr, -(-3 * quarter // 8) * 8, LANES), f32),
             pltpu.VMEM((nr, blocks, tile, LANES), bf16),
             pltpu.VMEM((nr, blocks, tile, LANES), bf16),
-            pltpu.VMEM((nr, slice_bins, LANES), f32),
-            pltpu.VMEM((nr, slice_bins, LANES), f32),
+            pltpu.VMEM((halves, nr, slice_bins // halves, LANES), f32),
+            pltpu.VMEM((halves, nr, slice_bins // halves, LANES), f32),
             pltpu.VMEM((groups, GROUP * HIGH * CHANNELS, GROUP * LOW), f32),
-            pltpu.VMEM((HIGH, LANES, LANES), f32),
+            pltpu.VMEM((halves, HIGH, LANES, LANES), f32),
             pltpu.VMEM((all_rows, LANES), f32),
             pltpu.VMEM((all_rows, LANES), jnp.int32),
             pltpu.VMEM((all_rows, LANES), f32),
@@ -391,8 +430,8 @@
             pltpu.SemaphoreType.DMA,
             pltpu.SemaphoreType.DMA((nr,)),
             pltpu.SemaphoreType.DMA((nr,)),
-            pltpu.SemaphoreType.DMA((nr,)),
-            pltpu.SemaphoreType.DMA((nr,)),
+            pltpu.SemaphoreType.DMA((halves, nr)),
+            pltpu.SemaphoreType.DMA((halves, nr)),
         ],
         compiler_params=pltpu.CompilerParams(
             collective_id=0, has_side_effects=True, vmem_limit_bytes=63 * 1024 * 1024
@@ -404,6 +443,15 @@
         node_ids.reshape(blocks, LANES),
         bin_index,
     )
+    hbm = pl.BlockSpec(memory_space=pltpu.HBM)
+    gradient, hessian, gain = pl.pallas_call(
+        hand_on,
+        out_shape=tuple(jax.ShapeDtypeStruct(a.shape, a.dtype) for a in results),
+        in_specs=[hbm] * 3,
+        out_specs=(hbm,) * 3,
+        scratch_shapes=[pltpu.SemaphoreType.DMA((3,))],
+        compiler_params=pltpu.CompilerParams(vmem_limit_bytes=63 * 1024 * 1024),
+    )(*results)
     return gradient.reshape(length), hessian.reshape(length), gain.transpose(0, 2, 1)
 
 

time: 41.7 us -> 43.9 us (1.053)
  Pallas kernels: 37.4 us -> 43.1 us
  local copies, waits for them, and re-layouts: 3.47 us -> 0 us
    pallas_call x0 -> x1, Pallas kernels: none -> 5.22 us  [shards(): pl.pallas_call(hand_on, out_shape=tuple((jax.ShapeDtypeStruct(a.shape, a....]
    unnamed x7 -> x0, local copies, waits for them, and re-layouts: 3.47 us -> none
    pallas_call x1, Pallas kernels: 37.4 us -> 37.9 us  [shards(): pl.pallas_call(functools.partial(kernel, nr, nf), out_shape=(jax.ShapeDty...]
where the time goes in v4:
time: 43.9 us; the launch traced here: 43.7 us
  Pallas kernels  43.1 us (98%)
  between operations  0.64 us (1%)
    pallas_call x1, Pallas kernels, shards(): pl.pallas_call(functools.partial(kernel, nr, nf), out_shape=(jax.ShapeDty...  37.9 us
    pallas_call x1, Pallas kernels, shards(): pl.pallas_call(hand_on, out_shape=tuple((jax.ShapeDtypeStruct(a.shape, a....  5.22 us

profile of v4, /device:TPU:0, one launch (start us, length us, event | category | flops | bytes accessed | tf_op | source)
XLA Modules:
  0.0 43.7 jit_solution(11804865462028198066)
XLA Ops:
  0.6 37.9 %shard_map.76 = (f32[4,128]{1,0:T(4,128)}, f32[4,128]{1,0:T(4,128)}, f32[8,32,128]{2,1,0:T(8,128)}) custom-call(f32[4,128]{1,0:T(4,128)} %bitcast.8, s32[4,128]{1,0:T(4,128)} %bitcast.9, s32[4,128]{1,0:T(4,128)} %bitcast.10, s32[16,128]{1,0:T(8,128)} %bitcast.7, s32[128,2048]{1,0:T(8,128)} %bin_hbm.1), custom_call_target="tpu_custom_call" | custom-call | tf_op jit(solution)/shard_map/pallas_call | solution.py:396
  38.5 5.2 %shard_map.77 = (f32[4,128]{1,0:T(4,128)}, f32[4,128]{1,0:T(4,128)}, f32[8,32,128]{2,1,0:T(8,128)}) custom-call(f32[4,128]{1,0:T(4,128)} %get-tuple-element.9.refs_0_, f32[4,128]{1,0:T(4,128)} %get-tuple-element.10.refs_1_, f32[8,32,128]{2,1,0:T(8,128)} %get-tuple-element.11.refs_2_), custom_call_target="tpu_custom_call" | custom-call | tf_op jit(solution)/shard_map/pallas_call | solution.py:447

commit v5 on v4

--- a/solution.py
+++ b/solution.py
@@ -181,12 +181,6 @@
 
     lax.fori_loop(0, blocks, pack, 0)
 
-    def send_bins(place, carry):
-        bin_copy(step_of(place, nr)).start()
-        return carry
-
-    lax.fori_loop(1, nr, send_bins, 0)
-
     bin_recv[my_row] = bin_send[my_row]
     acc[...] = jnp.zeros_like(acc)
 
@@ -199,6 +193,12 @@
         return carry
 
     lax.fori_loop(1, nf, send_feat, 0)
+
+    def send_bins(place, carry):
+        bin_copy(step_of(place, nr)).start()
+        return carry
+
+    lax.fori_loop(1, nr, send_bins, 0)
     pltpu.make_async_copy(feat_bytes, feat_bytes, feat_sem).wait()
 
     def spread(row, carry):
@@ -369,14 +369,20 @@
 
 
 def hand_on(*refs):
-    count = len(refs) // 2
-    copies = [
-        pltpu.make_async_copy(refs[place], refs[count + place], refs[-1].at[place]) for place in range(count)
-    ]
-    for copy in copies:
-        copy.start()
-    for copy in copies:
-        copy.wait()
+    count = len(refs) // 3
+    sems = refs[-1]
+    reads, writes = [], []
+    for place in range(count):
+        source, target, held = refs[place], refs[count + place], refs[2 * count + place]
+        reads.append(pltpu.make_async_copy(source, held, sems.at[0, place]))
+        writes.append(pltpu.make_async_copy(held, target, sems.at[1, place]))
+    for read in reads:
+        read.start()
+    for read, write in zip(reads, writes):
+        read.wait()
+        write.start()
+    for write in writes:
+        write.wait()
 
 
 def shards(nr, nf, predictor, events, tie_groups, node_ids, bin_index):
@@ -390,7 +396,7 @@
     groups = -(-own // GROUP)
     all_rows = nr * blocks
     slice_bins = BINS // nr
-    halves = 2 if own % (2 * GROUP) == 0 and NODES * own == LANES and slice_bins % 16 == 0 else 1
+    halves = 1
     vmem = pl.BlockSpec(memory_space=pltpu.VMEM)
     f32, bf16 = jnp.float32, jnp.bfloat16
     results = pl.pallas_call(
@@ -449,7 +455,7 @@
         out_shape=tuple(jax.ShapeDtypeStruct(a.shape, a.dtype) for a in results),
         in_specs=[hbm] * 3,
         out_specs=(hbm,) * 3,
-        scratch_shapes=[pltpu.SemaphoreType.DMA((3,))],
+        scratch_shapes=[pltpu.VMEM(a.shape, a.dtype) for a in results] + [pltpu.SemaphoreType.DMA((2, 3))],
         compiler_params=pltpu.CompilerParams(vmem_limit_bytes=63 * 1024 * 1024),
     )(*results)
     return gradient.reshape(length), hessian.reshape(length), gain.transpose(0, 2, 1)

time: 43.9 us -> 37.5 us (0.85)
  Pallas kernels: 43.1 us -> 36.7 us
    pallas_call x1, Pallas kernels: 5.22 us -> 1.62 us  [shards(): pl.pallas_call(hand_on, out_shape=tuple((jax.ShapeDtypeStruct(a.shape, a....]
    pallas_call x1, Pallas kernels: 37.9 us -> 35 us  [shards(): pl.pallas_call(functools.partial(kernel, nr, nf), out_shape=(jax.ShapeDty...]
where the time goes in v5:
time: 37.5 us; the launch traced here: 37.3 us
  Pallas kernels  36.7 us (98%)
  between operations  0.64 us (2%)
    pallas_call x1, Pallas kernels, shards(): pl.pallas_call(functools.partial(kernel, nr, nf), out_shape=(jax.ShapeDty...  35 us
    pallas_call x1, Pallas kernels, shards(): pl.pallas_call(hand_on, out_shape=tuple((jax.ShapeDtypeStruct(a.shape, a....  1.62 us

profile of v5, /device:TPU:0, one launch (start us, length us, event | category | flops | bytes accessed | tf_op | source)
XLA Modules:
  0.0 37.3 jit_solution(8427463207188846531)
XLA Ops:
  0.6 35.0 %shard_map.76 = (f32[4,128]{1,0:T(4,128)}, f32[4,128]{1,0:T(4,128)}, f32[8,32,128]{2,1,0:T(8,128)}) custom-call(f32[4,128]{1,0:T(4,128)} %bitcast.8, s32[4,128]{1,0:T(4,128)} %bitcast.9, s32[4,128]{1,0:T(4,128)} %bitcast.10, s32[16,128]{1,0:T(8,128)} %bitcast.7, s32[128,2048]{1,0:T(8,128)} %bin_hbm.1), custom_call_target="tpu_custom_call" | custom-call | tf_op jit(solution)/shard_map/pallas_call | solution.py:402
  35.7 1.6 %shard_map.77 = (f32[4,128]{1,0:T(4,128)}, f32[4,128]{1,0:T(4,128)}, f32[8,32,128]{2,1,0:T(8,128)}) custom-call(f32[4,128]{1,0:T(4,128)} %get-tuple-element.9.refs_0_, f32[4,128]{1,0:T(4,128)} %get-tuple-element.10.refs_1_, f32[8,32,128]{2,1,0:T(8,128)} %get-tuple-element.11.refs_2_), custom_call_target="tpu_custom_call" | custom-call | tf_op jit(solution)/shard_map/pallas_call | solution.py:453

commit v6 on v5

--- a/solution.py
+++ b/solution.py
@@ -15,6 +15,7 @@
 CHANNELS = 2 * NODES
 GROUP = 2
 BLOCKS = 8
+EARLY = 2
 MESH = pl.DeviceIdType.MESH
 EXACT = lax.Precision.HIGHEST
 
@@ -26,15 +27,6 @@
         other = other + ((step // bit) % 2) * bit * (1 - 2 * ((me // bit) % 2))
         bit *= 2
     return other
-
-
-def step_of(place, count):
-    half = count // 2
-    odd = place % 2
-    last = place // (count - 1)
-    later = (place + count - 1) // count
-    by_turns = odd * ((place + 1) // 2) + (1 - odd) * later * (half + place // 2 - 1)
-    return (1 - last) * by_turns + last * (count - 1)
 
 
 def triangle(rows, columns, keep):
@@ -181,6 +173,14 @@
 
     lax.fori_loop(0, blocks, pack, 0)
 
+    early = min(EARLY, nr - 1)
+
+    def send_bins(step, carry):
+        bin_copy(step).start()
+        return carry
+
+    lax.fori_loop(1, early + 1, send_bins, 0)
+
     bin_recv[my_row] = bin_send[my_row]
     acc[...] = jnp.zeros_like(acc)
 
@@ -194,11 +194,7 @@
 
     lax.fori_loop(1, nf, send_feat, 0)
 
-    def send_bins(place, carry):
-        bin_copy(step_of(place, nr)).start()
-        return carry
-
-    lax.fori_loop(1, nr, send_bins, 0)
+    lax.fori_loop(early + 1, nr, send_bins, 0)
     pltpu.make_async_copy(feat_bytes, feat_bytes, feat_sem).wait()
 
     def spread(row, carry):
@@ -229,11 +225,10 @@
     width = NODES * some
     short = slice_bins // halves
 
-    def prepare(place, carry):
-        step = step_of(place, nr)
+    def prepare(step):
         source = partner(my_row, step, nr)
 
-        @pl.when(place > 0)
+        @pl.when(step > 0)
         def _():
             bin_copy(step).wait_recv()
 
@@ -253,8 +248,7 @@
             high = jnp.floor(bins * (1.0 / LOW))
             highs[block] = high
             lows[block] = bins - high * LOW
-        count_source(source, 0)
-        return carry
+        return source
 
     def count_source(source, half):
         def one_chunk(chunk, carry):
@@ -292,8 +286,10 @@
 
         lax.fori_loop(0, blocks // BLOCKS, one_chunk, 0)
 
-    def count_again(half, source, carry):
-        count_source(source, half)
+    def count_all(step, carry):
+        source = prepare(step)
+        for half in range(halves):
+            count_source(source, half)
         return carry
 
     def send_gain(half, step, carry):
@@ -345,11 +341,10 @@
                         half, source, :, lanes : lanes + some
                     ]
 
+    lax.fori_loop(0, nr - 1, count_all, 0)
+    last = prepare(jnp.int32(nr - 1))
     for half in range(halves):
-        if half:
-            lax.fori_loop(0, nr, functools.partial(count_again, half), 0)
-        else:
-            lax.fori_loop(0, nr, prepare, 0)
+        count_source(last, half)
         split(half)
         lax.fori_loop(1, nr, functools.partial(send_gain, half), 0)
         gain_recv[half, my_row] = gain_send[half, my_row]
@@ -396,7 +391,7 @@
     groups = -(-own // GROUP)
     all_rows = nr * blocks
     slice_bins = BINS // nr
-    halves = 1
+    halves = 2 if own % (2 * GROUP) == 0 and NODES * own == LANES and slice_bins % 16 == 0 else 1
     vmem = pl.BlockSpec(memory_space=pltpu.VMEM)
     f32, bf16 = jnp.float32, jnp.bfloat16
     results = pl.pallas_call(

time: 37.5 us -> 39.3 us (1.048)
  Pallas kernels: 36.7 us -> 38.5 us
    pallas_call x1, Pallas kernels: 35 us -> 36.9 us  [shards(): pl.pallas_call(functools.partial(kernel, nr, nf), out_shape=(jax.ShapeDty...]
where the time goes in v6:
time: 39.3 us; the launch traced here: 39.2 us
  Pallas kernels  38.5 us (98%)
  between operations  0.64 us (2%)
    pallas_call x1, Pallas kernels, shards(): pl.pallas_call(functools.partial(kernel, nr, nf), out_shape=(jax.ShapeDty...  36.9 us
    pallas_call x1, Pallas kernels, shards(): pl.pallas_call(hand_on, out_shape=tuple((jax.ShapeDtypeStruct(a.shape, a....  1.62 us

profile of v6, /device:TPU:0, one launch (start us, length us, event | category | flops | bytes accessed | tf_op | source)
XLA Modules:
  0.0 39.2 jit_solution(3956040887347490951)
XLA Ops:
  0.6 36.9 %shard_map.76 = (f32[4,128]{1,0:T(4,128)}, f32[4,128]{1,0:T(4,128)}, f32[8,32,128]{2,1,0:T(8,128)}) custom-call(f32[4,128]{1,0:T(4,128)} %bitcast.8, s32[4,128]{1,0:T(4,128)} %bitcast.9, s32[4,128]{1,0:T(4,128)} %bitcast.10, s32[16,128]{1,0:T(8,128)} %bitcast.7, s32[128,2048]{1,0:T(8,128)} %bin_hbm.1), custom_call_target="tpu_custom_call" | custom-call | tf_op jit(solution)/shard_map/pallas_call | solution.py:397
  37.5 1.6 %shard_map.77 = (f32[4,128]{1,0:T(4,128)}, f32[4,128]{1,0:T(4,128)}, f32[8,32,128]{2,1,0:T(8,128)}) custom-call(f32[4,128]{1,0:T(4,128)} %get-tuple-element.9.refs_0_, f32[4,128]{1,0:T(4,128)} %get-tuple-element.10.refs_1_, f32[8,32,128]{2,1,0:T(8,128)} %get-tuple-element.11.refs_2_), custom_call_target="tpu_custom_call" | custom-call | tf_op jit(solution)/shard_map/pallas_call | solution.py:448

commit v7 on v5

--- a/solution.py
+++ b/solution.py
@@ -16,7 +16,6 @@
 GROUP = 2
 BLOCKS = 8
 MESH = pl.DeviceIdType.MESH
-EXACT = lax.Precision.HIGHEST
 
 
 def partner(me, step, count):
@@ -40,11 +39,32 @@
 def triangle(rows, columns, keep):
     a = lax.broadcasted_iota(jnp.int32, (rows, columns), 0)
     b = lax.broadcasted_iota(jnp.int32, (rows, columns), 1)
-    return keep(a, b).astype(jnp.float32)
-
-
-def exact_dot(a, b):
-    return jnp.dot(a, b, precision=EXACT, preferred_element_type=jnp.float32)
+    return keep(a, b).astype(jnp.float32).astype(jnp.bfloat16)
+
+
+def thirds(value):
+    parts = []
+    for _ in range(3):
+        part = value.astype(jnp.bfloat16)
+        parts.append(part)
+        value = value - part.astype(jnp.float32)
+    return parts
+
+
+def sum_lanes(values, keep):
+    rows = values[0].shape[0]
+    stacked = jnp.concatenate([part for value in values for part in thirds(value)], axis=0)
+    product = jnp.dot(stacked, triangle(LANES, LANES, keep), preferred_element_type=jnp.float32)
+    pieces = [product[place * rows : (place + 1) * rows] for place in range(3 * len(values))]
+    return [pieces[3 * k] + (pieces[3 * k + 1] + pieces[3 * k + 2]) for k in range(len(values))]
+
+
+def sum_rows(values, keep):
+    rows = values[0].shape[0]
+    stacked = jnp.concatenate([part for value in values for part in thirds(value)], axis=1)
+    product = jnp.dot(triangle(rows, rows, keep), stacked, preferred_element_type=jnp.float32)
+    pieces = [product[:, place * LANES : (place + 1) * LANES] for place in range(3 * len(values))]
+    return [pieces[3 * k] + (pieces[3 * k + 1] + pieces[3 * k + 2]) for k in range(len(values))]
 
 
 def fill(value, known, step):
@@ -63,22 +83,17 @@
     lane = lax.broadcasted_iota(jnp.int32, (rows, LANES), 1)
     begins = ((lane % 8 == 0) | (tie != pltpu.roll(tie, 1, 1))).astype(jnp.float32)
     finish = pltpu.roll(begins, LANES - 1, 1)
-    lane_suffix = exact_dot(hazard_exp, triangle(LANES, LANES, lambda a, b: a >= b))
-    whole = jnp.broadcast_to(lane_suffix[:, :1], (rows, LANES))
-    suffix = lane_suffix + exact_dot(triangle(rows, rows, lambda a, b: b > a), whole)
+    (lane_suffix,) = sum_lanes([hazard_exp], lambda a, b: a >= b)
+    (later,) = sum_rows([jnp.broadcast_to(lane_suffix[:, :1], (rows, LANES))], lambda a, b: b > a)
+    suffix = lane_suffix + later
     risk_sum = fill(suffix, begins, 1)
     weight_one = failed / risk_sum
     weight_two = failed / (risk_sum * risk_sum)
-    upper = triangle(LANES, LANES, lambda a, b: a <= b)
-    earlier = triangle(rows, rows, lambda a, b: b < a)
-
-    def running(weight):
-        within = exact_dot(weight, upper)
-        whole = jnp.broadcast_to(within[:, LANES - 1 :], (rows, LANES))
-        return fill(within + exact_dot(earlier, whole), finish, -1)
-
-    hazard_one = running(weight_one)
-    hazard_two = running(weight_two)
+    within = sum_lanes([weight_one, weight_two], lambda a, b: a <= b)
+    wholes = [jnp.broadcast_to(w[:, LANES - 1 :], (rows, LANES)) for w in within]
+    before = sum_rows(wholes, lambda a, b: b < a)
+    hazard_one = fill(within[0] + before[0], finish, -1)
+    hazard_two = fill(within[1] + before[1], finish, -1)
     gradient = hazard_exp * hazard_one - failed
     hessian = hazard_exp * hazard_one - hazard_exp * hazard_exp * hazard_two
     return gradient, hessian

time: 37.5 us -> 37.3 us (level)
  no operation moved by 1% of the time
where the time goes in v7:
time: 37.3 us; the launch traced here: 37.1 us
  Pallas kernels  36.5 us (98%)
  between operations  0.64 us (2%)
    pallas_call x1, Pallas kernels, shards(): pl.pallas_call(functools.partial(kernel, nr, nf), out_shape=(jax.ShapeDty...  34.8 us
    pallas_call x1, Pallas kernels, shards(): pl.pallas_call(hand_on, out_shape=tuple((jax.ShapeDtypeStruct(a.shape, a....  1.62 us

profile of v7, /device:TPU:0, one launch (start us, length us, event | category | flops | bytes accessed | tf_op | source)
XLA Modules:
  0.0 37.1 jit_solution(10231707302221656303)
XLA Ops:
  0.6 34.8 %shard_map.76 = (f32[4,128]{1,0:T(4,128)}, f32[4,128]{1,0:T(4,128)}, f32[8,32,128]{2,1,0:T(8,128)}) custom-call(f32[4,128]{1,0:T(4,128)} %bitcast.8, s32[4,128]{1,0:T(4,128)} %bitcast.9, s32[4,128]{1,0:T(4,128)} %bitcast.10, s32[16,128]{1,0:T(8,128)} %bitcast.7, s32[128,2048]{1,0:T(8,128)} %bin_hbm.1), custom_call_target="tpu_custom_call" | custom-call | tf_op jit(solution)/shard_map/pallas_call | solution.py:417
  35.5 1.6 %shard_map.77 = (f32[4,128]{1,0:T(4,128)}, f32[4,128]{1,0:T(4,128)}, f32[8,32,128]{2,1,0:T(8,128)}) custom-call(f32[4,128]{1,0:T(4,128)} %get-tuple-element.9.refs_0_, f32[4,128]{1,0:T(4,128)} %get-tuple-element.10.refs_1_, f32[8,32,128]{2,1,0:T(8,128)} %get-tuple-element.11.refs_2_), custom_call_target="tpu_custom_call" | custom-call | tf_op jit(solution)/shard_map/pallas_call | solution.py:468

commit v8 on v7

--- a/solution.py
+++ b/solution.py
@@ -14,7 +14,7 @@
 LOW = BINS // HIGH
 CHANNELS = 2 * NODES
 GROUP = 2
-BLOCKS = 8
+BLOCKS = 16
 MESH = pl.DeviceIdType.MESH
 
 

time: 37.3 us -> 35.7 us (0.957)
  Pallas kernels: 36.5 us -> 34.9 us
    pallas_call x1, Pallas kernels: 34.8 us -> 33.3 us  [shards(): pl.pallas_call(functools.partial(kernel, nr, nf), out_shape=(jax.ShapeDty...]
where the time goes in v8:
time: 35.7 us; the launch traced here: 35.5 us
  Pallas kernels  34.9 us (98%)
  between operations  0.64 us (2%)
    pallas_call x1, Pallas kernels, shards(): pl.pallas_call(functools.partial(kernel, nr, nf), out_shape=(jax.ShapeDty...  33.3 us
    pallas_call x1, Pallas kernels, shards(): pl.pallas_call(hand_on, out_shape=tuple((jax.ShapeDtypeStruct(a.shape, a....  1.62 us

profile of v8, /device:TPU:0, one launch (start us, length us, event | category | flops | bytes accessed | tf_op | source)
XLA Modules:
  0.0 35.5 jit_solution(15658743961286372463)
XLA Ops:
  0.6 33.3 %shard_map.76 = (f32[4,128]{1,0:T(4,128)}, f32[4,128]{1,0:T(4,128)}, f32[8,32,128]{2,1,0:T(8,128)}) custom-call(f32[4,128]{1,0:T(4,128)} %bitcast.8, s32[4,128]{1,0:T(4,128)} %bitcast.9, s32[4,128]{1,0:T(4,128)} %bitcast.10, s32[16,128]{1,0:T(8,128)} %bitcast.7, s32[128,2048]{1,0:T(8,128)} %bin_hbm.1), custom_call_target="tpu_custom_call" | custom-call | tf_op jit(solution)/shard_map/pallas_call | solution.py:417
  33.9 1.6 %shard_map.77 = (f32[4,128]{1,0:T(4,128)}, f32[4,128]{1,0:T(4,128)}, f32[8,32,128]{2,1,0:T(8,128)}) custom-call(f32[4,128]{1,0:T(4,128)} %get-tuple-element.9.refs_0_, f32[4,128]{1,0:T(4,128)} %get-tuple-element.10.refs_1_, f32[8,32,128]{2,1,0:T(8,128)} %get-tuple-element.11.refs_2_), custom_call_target="tpu_custom_call" | custom-call | tf_op jit(solution)/shard_map/pallas_call | solution.py:468
